TPU v7x, 32 devices: a whole 2x2x4 slice. The times are simulated.
32 devices in a mesh: section: 4 (over y, core), ctx: 8 (over z, x).
Axes of the slice: x: 2, y: 2, z: 4, core: 2. Of those that a mesh axis runs over, the one named last changes fastest.
Arguments:
- query_rows: bfloat16 [4096, 4096], P(('section', 'ctx')), may hold values from -6 to 6
- key_rows: bfloat16 [4096, 4096], P(('section', 'ctx')), may hold values from -6 to 6
- value_rows: bfloat16 [4096, 4096], P(('section', 'ctx')), may hold values from -6 to 6
- short_taps: bfloat16 [4, 3, 3, 4096], P('section', None, None, 'ctx'), may hold values from -3 to 3
- long_taps: bfloat16 [4, 4096, 128], P('section', 'ctx'), may hold values from -0.5 to 0.5
- skip_gain: bfloat16 [4, 4096], P('section', 'ctx'), may hold values from 0.5 to 1.5
- prior_qkv: bfloat16 [4, 3, 2, 4096], P('section', None, None, 'ctx'), may hold values from -6 to 6
- prior_product: bfloat16 [4, 127, 4096], P('section', None, 'ctx'), may hold values from -6 to 6
Outputs:
- handed: bfloat16 [4096, 4096], P(('section', 'ctx'))
All inputs are finite; a program needn't handle non-finite values.
Results may differ from a plain program's by a relative error of at most 0.005.
Values may be sent and summed in bfloat16 or wider, within the bound.
A program may use at most 128 MiB of HBM per device.

v0:
```python
import jax
import jax.numpy as jnp
from jax import lax
from jax.sharding import PartitionSpec as P


def passed_along(value, axis, steps):
    count = lax.axis_size(axis)
    pairs = [(source, (source + steps) % count) for source in range(count)]
    return lax.ppermute(value, axis, pairs)


def featurize(rows, history, taps):
    padded = jnp.concatenate([history, rows], axis=0).astype(jnp.float32)
    weights = taps.astype(jnp.float32)
    return weights[0] * padded[2:] + weights[1] * padded[1:-1] + weights[2] * padded[:-2]


def causal_filter(product, history, tap_rows):
    count, width = product.shape
    blocks = count // 128
    group = min(width, 128)
    groups = width // group
    padded = jnp.concatenate([jnp.zeros((1, width), product.dtype), history, product], axis=0)
    lower_rows = padded[:count].reshape(blocks, 128, groups, group).transpose(2, 0, 1, 3)
    upper_rows = padded[128:].reshape(blocks, 128, groups, group).transpose(2, 0, 1, 3)
    reversed_taps = tap_rows[:, ::-1]
    skewed = jnp.concatenate(
        [
            jnp.zeros((width, 1), tap_rows.dtype),
            reversed_taps,
            jnp.zeros((width, 128), tap_rows.dtype),
        ],
        axis=1,
    )
    skewed = skewed.reshape(groups, group, 257)

    def one_group(pieces):
        group_taps, lower_part, upper_part = pieces
        tiled = jnp.tile(group_taps, (1, 128))[:, : 128 * 256]
        toeplitz = tiled.reshape(group, 128, 256)
        own_part = jnp.einsum(
            "cij,bjc->bic", toeplitz[:, :, :128], lower_part, preferred_element_type=jnp.float32
        )
        prior_part = jnp.einsum(
            "cij,bjc->bic", toeplitz[:, :, 128:], upper_part, preferred_element_type=jnp.float32
        )
        return own_part + prior_part

    result = lax.map(one_group, (skewed, lower_rows, upper_rows))
    return result.transpose(1, 2, 0, 3).reshape(count, width)


def mixer(query_rows, key_rows, value_rows, edges, short_set, tap_rows, gain_row, send_tail):
    query_feat = featurize(query_rows, edges[0], short_set[0])
    key_feat = featurize(key_rows, edges[1], short_set[1])
    value_feat = featurize(value_rows, edges[2], short_set[2])
    product = (key_feat * value_feat).astype(jnp.bfloat16)
    history = send_tail(product)
    filtered = causal_filter(product, history, tap_rows)
    mixed = query_feat * (filtered + gain_row.astype(jnp.float32) * product.astype(jnp.float32))
    return mixed.astype(jnp.bfloat16)


def body(
    query_rows, key_rows, value_rows, short_taps, long_taps, skip_gain, prior_qkv, prior_product
):
    seq_query, seq_key, seq_value = (
        lax.all_to_all(query_rows, "ctx", split_axis=1, concat_axis=0, tiled=True),
        lax.all_to_all(key_rows, "ctx", split_axis=1, concat_axis=0, tiled=True),
        lax.all_to_all(value_rows, "ctx", split_axis=1, concat_axis=0, tiled=True),
    )
    own_prior = prior_qkv[0]

    def prior_tail(product):
        return prior_product[0]

    mixed = mixer(
        seq_query,
        seq_key,
        seq_value,
        (own_prior[0], own_prior[1], own_prior[2]),
        short_taps[0],
        long_taps[0],
        skip_gain[0],
        prior_tail,
    )
    rows_out = lax.all_to_all(mixed, "ctx", split_axis=0, concat_axis=1, tiled=True)
    return passed_along(rows_out, "section", 1)


def solution(mesh):
    in_specs = (
        P(("section", "ctx"), None),
        P(("section", "ctx"), None),
        P(("section", "ctx"), None),
        P("section", None, None, "ctx"),
        P("section", "ctx", None),
        P("section", "ctx"),
        P("section", None, None, "ctx"),
        P("section", None, "ctx"),
    )
    out_specs = P(("section", "ctx"), None)
    return jax.shard_map(body, mesh=mesh, in_specs=in_specs, out_specs=out_specs, check_vma=False)
```

profile of v0, /device:TPU:0, one launch (start us, length us, event | category | flops | bytes accessed | tf_op | source)
XLA Modules:
  0.0 325.3 jit_solution(8257831593725057964)
XLA Ops:
  0.0 2.4 copy.50
  2.4 7.3 %all-to-all-start.1 = ((bf16[128,8,512]{2,0,1:T(8,128)(2,1)}), bf16[128,8,512]{2,0,1:T(8,128)(2,1)S(1)}, u32[]{:S(2)}, u32[]{:S(2)}) async-start(bf16[128,8,512]{2,0,1:T(8,128)(2,1)} %bitcast.71), calls=%async_computation.1 | async-start | bytes 2097152 | tf_op jit(solution)/shard_map/all_to_all | solution.py:70
  10.8 24.6 %all-to-all-done.1 = bf16[128,8,512]{2,0,1:T(8,128)(2,1)S(1)} async-done(((bf16[128,8,512]{2,0,1:T(8,128)(2,1)}), bf16[128,8,512]{2,0,1:T(8,128)(2,1)S(1)}, u32[]{:S(2)}, u32[]{:S(2)}) %all-to-all-start.1) | async-done | bytes 1048608 | tf_op jit(solution)/shard_map/all_to_all | solution.py:70
  35.4 3.6 %all-to-all-start.2 = ((bf16[128,8,512]{2,0,1:T(8,128)(2,1)}), bf16[128,8,512]{2,0,1:T(8,128)(2,1)S(1)}, u32[]{:S(2)}, u32[]{:S(2)}) async-start(bf16[128,8,512]{2,0,1:T(8,128)(2,1)} %bitcast.70), calls=%async_computation.2 | async-start | bytes 2097152 | tf_op jit(solution)/shard_map/all_to_all | solution.py:71
  39.9 2.3 copy.51
  43.9 21.1 %all-to-all-done.2 = bf16[128,8,512]{2,0,1:T(8,128)(2,1)S(1)} async-done(((bf16[128,8,512]{2,0,1:T(8,128)(2,1)}), bf16[128,8,512]{2,0,1:T(8,128)(2,1)S(1)}, u32[]{:S(2)}, u32[]{:S(2)}) %all-to-all-start.2) | async-done | bytes 1048608 | tf_op jit(solution)/shard_map/all_to_all | solution.py:71
  64.9 4.2 %all-to-all-start = ((bf16[128,8,512]{2,0,1:T(8,128)(2,1)}), bf16[128,8,512]{2,0,1:T(8,128)(2,1)}, u32[]{:S(2)}, u32[]{:S(2)}) async-start(bf16[128,8,512]{2,0,1:T(8,128)(2,1)} %bitcast.72), calls=%async_computation | async-start | bytes 2097152 | tf_op jit(solution)/shard_map/all_to_all | solution.py:69
  73.6 2.1 reshape.65
  75.8 2.0 copy.27
  77.8 3.0 copy.29
  80.8 190.9 %while.10 = (s32[]{:T(128)}, f32[4,8,128,128]{2,1,3,0:T(8,128)}, bf16[4,8,128,128]{2,1,3,0:T(8,128)(2,1)S(1)}, bf16[4,128,257]{1,2,0:T(8,128)(2,1)S(1)}, bf16[4,8,128,128]{2,1,3,0:T(8,128)(2,1)}, /*index=5*/s32[]{:T(128)}) while((s32[]{:T(128)}, f32[4,8,128,128]{2,1,3,0:T(8,128)}, bf16[4,8,128,128]{2,1,3,0:T(8,128)(2,1)S(1)}, ...), condition=%wide.region_1.2_spmd, body=%wide.region_0.1_spmd.sunk | while | flops 67239936 | bytes 94668648 | solution.py:50
  80.8 4.5 %tile.13 = bf16[128,128,257]{0,2,1:T(8,128)(2,1)} broadcast(bf16[128,257]{0,1:T(8,128)(2,1)S(1)} %dynamic-slice_bitcast_fusion.2), dimensions={0,2} | broadcast | bytes 8487168 | tf_op jit(solution)/shard_map/while/body/eval_jaxpr/tile | solution.py:40
  85.2 12.9 %tile.14 = bf16[128,32896]{0,1:T(8,128)(2,1)} reshape(bf16[128,128,257]{0,2,1:T(8,128)(2,1)} %tile.13) | data formatting | bytes 16842752 | tf_op jit(solution)/shard_map/while/body/eval_jaxpr/tile | solution.py:40
  98.2 3.4 %slice-done = bf16[128,32768]{0,1:T(8,128)(2,1)S(1)} async-done(((bf16[128,32896]{0,1:T(8,128)(2,1)}), bf16[128,32768]{0,1:T(8,128)(2,1)S(1)}, s32[]{:S(2)}) %slice-start) | async-done | bytes 8388632 | tf_op jit(solution)/shard_map/while/body/eval_jaxpr/slice | solution.py:40
  101.5 3.8 %fusion.36 = (bf16[128,128,128]{0,2,1:T(8,128)(2,1)}, bf16[128,128,128]{0,2,1:T(8,128)(2,1)}) fusion(bf16[128,128,256]{0,2,1:T(8,128)(2,1)S(1)} %bitcast.87), kind=kLoop, calls=%fused_computation.44.clone.1 | loop fusion | bytes 16777216 | tf_op jit(solution)/shard_map/while/body/eval_jaxpr/slice | solution.py:46
  105.3 6.6 %copy.54 = bf16[128,128,128]{2,1,0:T(8,128)(2,1)} copy(bf16[128,128,128]{0,2,1:T(8,128)(2,1)} %get-tuple-element.101) | data formatting | bytes 8388608 | tf_op jit(solution)/shard_map/while
  111.9 4.4 %fusion.37 = f32[128,8,128]{2,1,0:T(8,128)S(1)} fusion(bf16[128,128,128]{2,1,0:T(8,128)(2,1)} %copy.54, bf16[4,8,128,128]{2,1,3,0:T(8,128)(2,1)S(1)} %get-tuple-element.117, s32[]{:T(128)} %get-tuple-element.109), kind=kOutput, calls=%fused_computation.4.clone.1 | convolution fusion | flops 33554432 | bytes 4980740 | tf_op jit(solution)/shard_map/while/body/eval_jaxpr/cij,bjc->bic/dot_general | solution.py:42
  116.4 6.8 %copy.55 = bf16[128,128,128]{2,1,0:T(8,128)(2,1)} copy(bf16[128,128,128]{0,2,1:T(8,128)(2,1)} %get-tuple-element.102) | data formatting | bytes 8388608 | tf_op jit(solution)/shard_map/while
  123.2 5.3 %fusion.38 = f32[4,8,128,128]{2,1,3,0:T(8,128)} fusion(f32[4,8,128,128]{2,1,3,0:T(8,128)} %get-tuple-element.110, s32[]{:T(128)} %get-tuple-element.109, f32[128,8,128]{2,1,0:T(8,128)S(1)} %fusion.37, bf16[128,128,128]{2,1,0:T(8,128)(2,1)} %copy.55, bf16[4,8,128,128]{2,1,3,0:T(8,128)(2,1)} %get-tuple-element.119), kind=kOutput, calls=%fused_computation.2.clone.1 | convolution fusion | flops 33685504 | bytes 5506048 | tf_op jit(solution)/shard_map/while/body/eval_jaxpr/cij,bjc->bic/dot_general | solution.py:45
  128.5 4.5 %tile.13 = bf16[128,128,257]{0,2,1:T(8,128)(2,1)} broadcast(bf16[128,257]{0,1:T(8,128)(2,1)S(1)} %dynamic-slice_bitcast_fusion.2), dimensions={0,2} | broadcast | bytes 8487168 | tf_op jit(solution)/shard_map/while/body/eval_jaxpr/tile | solution.py:40
  133.0 12.9 %tile.14 = bf16[128,32896]{0,1:T(8,128)(2,1)} reshape(bf16[128,128,257]{0,2,1:T(8,128)(2,1)} %tile.13) | data formatting | bytes 16842752 | tf_op jit(solution)/shard_map/while/body/eval_jaxpr/tile | solution.py:40
  145.9 3.4 %slice-done = bf16[128,32768]{0,1:T(8,128)(2,1)S(1)} async-done(((bf16[128,32896]{0,1:T(8,128)(2,1)}), bf16[128,32768]{0,1:T(8,128)(2,1)S(1)}, s32[]{:S(2)}) %slice-start) | async-done | bytes 8388632 | tf_op jit(solution)/shard_map/while/body/eval_jaxpr/slice | solution.py:40
  149.3 3.8 %fusion.36 = (bf16[128,128,128]{0,2,1:T(8,128)(2,1)}, bf16[128,128,128]{0,2,1:T(8,128)(2,1)}) fusion(bf16[128,128,256]{0,2,1:T(8,128)(2,1)S(1)} %bitcast.87), kind=kLoop, calls=%fused_computation.44.clone.1 | loop fusion | bytes 16777216 | tf_op jit(solution)/shard_map/while/body/eval_jaxpr/slice | solution.py:46
  153.0 6.6 %copy.54 = bf16[128,128,128]{2,1,0:T(8,128)(2,1)} copy(bf16[128,128,128]{0,2,1:T(8,128)(2,1)} %get-tuple-element.101) | data formatting | bytes 8388608 | tf_op jit(solution)/shard_map/while
  159.7 4.4 %fusion.37 = f32[128,8,128]{2,1,0:T(8,128)S(1)} fusion(bf16[128,128,128]{2,1,0:T(8,128)(2,1)} %copy.54, bf16[4,8,128,128]{2,1,3,0:T(8,128)(2,1)S(1)} %get-tuple-element.117, s32[]{:T(128)} %get-tuple-element.109), kind=kOutput, calls=%fused_computation.4.clone.1 | convolution fusion | flops 33554432 | bytes 4980740 | tf_op jit(solution)/shard_map/while/body/eval_jaxpr/cij,bjc->bic/dot_general | solution.py:42
  164.1 6.8 %copy.55 = bf16[128,128,128]{2,1,0:T(8,128)(2,1)} copy(bf16[128,128,128]{0,2,1:T(8,128)(2,1)} %get-tuple-element.102) | data formatting | bytes 8388608 | tf_op jit(solution)/shard_map/while
  170.9 5.4 %fusion.38 = f32[4,8,128,128]{2,1,3,0:T(8,128)} fusion(f32[4,8,128,128]{2,1,3,0:T(8,128)} %get-tuple-element.110, s32[]{:T(128)} %get-tuple-element.109, f32[128,8,128]{2,1,0:T(8,128)S(1)} %fusion.37, bf16[128,128,128]{2,1,0:T(8,128)(2,1)} %copy.55, bf16[4,8,128,128]{2,1,3,0:T(8,128)(2,1)} %get-tuple-element.119), kind=kOutput, calls=%fused_computation.2.clone.1 | convolution fusion | flops 33685504 | bytes 5506048 | tf_op jit(solution)/shard_map/while/body/eval_jaxpr/cij,bjc->bic/dot_general | solution.py:45
  176.2 4.5 %tile.13 = bf16[128,128,257]{0,2,1:T(8,128)(2,1)} broadcast(bf16[128,257]{0,1:T(8,128)(2,1)S(1)} %dynamic-slice_bitcast_fusion.2), dimensions={0,2} | broadcast | bytes 8487168 | tf_op jit(solution)/shard_map/while/body/eval_jaxpr/tile | solution.py:40
  180.7 12.9 %tile.14 = bf16[128,32896]{0,1:T(8,128)(2,1)} reshape(bf16[128,128,257]{0,2,1:T(8,128)(2,1)} %tile.13) | data formatting | bytes 16842752 | tf_op jit(solution)/shard_map/while/body/eval_jaxpr/tile | solution.py:40
  193.6 3.4 %slice-done = bf16[128,32768]{0,1:T(8,128)(2,1)S(1)} async-done(((bf16[128,32896]{0,1:T(8,128)(2,1)}), bf16[128,32768]{0,1:T(8,128)(2,1)S(1)}, s32[]{:S(2)}) %slice-start) | async-done | bytes 8388632 | tf_op jit(solution)/shard_map/while/body/eval_jaxpr/slice | solution.py:40
  197.0 3.8 %fusion.36 = (bf16[128,128,128]{0,2,1:T(8,128)(2,1)}, bf16[128,128,128]{0,2,1:T(8,128)(2,1)}) fusion(bf16[128,128,256]{0,2,1:T(8,128)(2,1)S(1)} %bitcast.87), kind=kLoop, calls=%fused_computation.44.clone.1 | loop fusion | bytes 16777216 | tf_op jit(solution)/shard_map/while/body/eval_jaxpr/slice | solution.py:46
  200.8 6.6 %copy.54 = bf16[128,128,128]{2,1,0:T(8,128)(2,1)} copy(bf16[128,128,128]{0,2,1:T(8,128)(2,1)} %get-tuple-element.101) | data formatting | bytes 8388608 | tf_op jit(solution)/shard_map/while
  207.4 4.4 %fusion.37 = f32[128,8,128]{2,1,0:T(8,128)S(1)} fusion(bf16[128,128,128]{2,1,0:T(8,128)(2,1)} %copy.54, bf16[4,8,128,128]{2,1,3,0:T(8,128)(2,1)S(1)} %get-tuple-element.117, s32[]{:T(128)} %get-tuple-element.109), kind=kOutput, calls=%fused_computation.4.clone.1 | convolution fusion | flops 33554432 | bytes 4980740 | tf_op jit(solution)/shard_map/while/body/eval_jaxpr/cij,bjc->bic/dot_general | solution.py:42
  211.8 6.8 %copy.55 = bf16[128,128,128]{2,1,0:T(8,128)(2,1)} copy(bf16[128,128,128]{0,2,1:T(8,128)(2,1)} %get-tuple-element.102) | data formatting | bytes 8388608 | tf_op jit(solution)/shard_map/while
  218.6 5.3 %fusion.38 = f32[4,8,128,128]{2,1,3,0:T(8,128)} fusion(f32[4,8,128,128]{2,1,3,0:T(8,128)} %get-tuple-element.110, s32[]{:T(128)} %get-tuple-element.109, f32[128,8,128]{2,1,0:T(8,128)S(1)} %fusion.37, bf16[128,128,128]{2,1,0:T(8,128)(2,1)} %copy.55, bf16[4,8,128,128]{2,1,3,0:T(8,128)(2,1)} %get-tuple-element.119), kind=kOutput, calls=%fused_computation.2.clone.1 | convolution fusion | flops 33685504 | bytes 5506048 | tf_op jit(solution)/shard_map/while/body/eval_jaxpr/cij,bjc->bic/dot_general | solution.py:45
  224.0 4.5 %tile.13 = bf16[128,128,257]{0,2,1:T(8,128)(2,1)} broadcast(bf16[128,257]{0,1:T(8,128)(2,1)S(1)} %dynamic-slice_bitcast_fusion.2), dimensions={0,2} | broadcast | bytes 8487168 | tf_op jit(solution)/shard_map/while/body/eval_jaxpr/tile | solution.py:40
  228.4 12.9 %tile.14 = bf16[128,32896]{0,1:T(8,128)(2,1)} reshape(bf16[128,128,257]{0,2,1:T(8,128)(2,1)} %tile.13) | data formatting | bytes 16842752 | tf_op jit(solution)/shard_map/while/body/eval_jaxpr/tile | solution.py:40
  241.3 3.4 %slice-done = bf16[128,32768]{0,1:T(8,128)(2,1)S(1)} async-done(((bf16[128,32896]{0,1:T(8,128)(2,1)}), bf16[128,32768]{0,1:T(8,128)(2,1)S(1)}, s32[]{:S(2)}) %slice-start) | async-done | bytes 8388632 | tf_op jit(solution)/shard_map/while/body/eval_jaxpr/slice | solution.py:40
  244.7 3.8 %fusion.36 = (bf16[128,128,128]{0,2,1:T(8,128)(2,1)}, bf16[128,128,128]{0,2,1:T(8,128)(2,1)}) fusion(bf16[128,128,256]{0,2,1:T(8,128)(2,1)S(1)} %bitcast.87), kind=kLoop, calls=%fused_computation.44.clone.1 | loop fusion | bytes 16777216 | tf_op jit(solution)/shard_map/while/body/eval_jaxpr/slice | solution.py:46
  248.5 6.6 %copy.54 = bf16[128,128,128]{2,1,0:T(8,128)(2,1)} copy(bf16[128,128,128]{0,2,1:T(8,128)(2,1)} %get-tuple-element.101) | data formatting | bytes 8388608 | tf_op jit(solution)/shard_map/while
  255.1 4.4 %fusion.37 = f32[128,8,128]{2,1,0:T(8,128)S(1)} fusion(bf16[128,128,128]{2,1,0:T(8,128)(2,1)} %copy.54, bf16[4,8,128,128]{2,1,3,0:T(8,128)(2,1)S(1)} %get-tuple-element.117, s32[]{:T(128)} %get-tuple-element.109), kind=kOutput, calls=%fused_computation.4.clone.1 | convolution fusion | flops 33554432 | bytes 4980740 | tf_op jit(solution)/shard_map/while/body/eval_jaxpr/cij,bjc->bic/dot_general | solution.py:42
  259.6 6.8 %copy.55 = bf16[128,128,128]{2,1,0:T(8,128)(2,1)} copy(bf16[128,128,128]{0,2,1:T(8,128)(2,1)} %get-tuple-element.102) | data formatting | bytes 8388608 | tf_op jit(solution)/shard_map/while
  266.4 5.4 %fusion.38 = f32[4,8,128,128]{2,1,3,0:T(8,128)} fusion(f32[4,8,128,128]{2,1,3,0:T(8,128)} %get-tuple-element.110, s32[]{:T(128)} %get-tuple-element.109, f32[128,8,128]{2,1,0:T(8,128)S(1)} %fusion.37, bf16[128,128,128]{2,1,0:T(8,128)(2,1)} %copy.55, bf16[4,8,128,128]{2,1,3,0:T(8,128)(2,1)} %get-tuple-element.119), kind=kOutput, calls=%fused_computation.2.clone.1 | convolution fusion | flops 33685504 | bytes 5506048 | tf_op jit(solution)/shard_map/while/body/eval_jaxpr/cij,bjc->bic/dot_general | solution.py:45
  271.7 2.1 copy.48
  273.8 1.8 copy.37
  275.6 1.7 maximum_convert_fusion
  278.5 30.6 %all_to_all.76 = bf16[8,128,512]{2,1,0:T(8,128)(2,1)S(1)} all-to-all(bf16[8,128,512]{2,1,0:T(8,128)(2,1)S(1)} %bitcast.91), channel_id=1, replica_groups=mesh['section'=4,'ctx'=8] {'ctx'}, dimensions={0} | all-to-all | bytes 2097152 | tf_op jit(solution)/shard_map/all_to_all | solution.py:88
  309.8 14.2 %collective-permute-done = bf16[128,4096]{0,1:T(8,128)(2,1)S(1)} collective-permute-done((bf16[128,4096]{0,1:T(8,128)(2,1)S(1)}, bf16[128,4096]{0,1:T(8,128)(2,1)S(1)}, u32[]{:S(2)}, u32[]{:S(2)}) %collective-permute-start) | collective-permute-done | bytes 1048608 | tf_op jit(solution)/shard_map/ppermute | solution.py:10
  (49 shorter events, 11.2 us)
Async XLA Ops:
  0.0 9.6 %copy-start.2 = (bf16[128,4096]{1,0:T(8,128)(2,1)S(1)}, bf16[128,4096]{1,0:T(8,128)(2,1)}, u32[]{:S(2)}) copy-start(bf16[128,4096]{1,0:T(8,128)(2,1)} %param.12) | copy-start | bytes 3145732
  2.4 33.0 %all-to-all-start.1 = ((bf16[128,8,512]{2,0,1:T(8,128)(2,1)}), bf16[128,8,512]{2,0,1:T(8,128)(2,1)S(1)}, u32[]{:S(2)}, u32[]{:S(2)}) async-start(bf16[128,8,512]{2,0,1:T(8,128)(2,1)} %bitcast.71), calls=%async_computation.1 | async-start | bytes 2097152 | tf_op jit(solution)/shard_map/all_to_all | solution.py:70
  9.6 29.4 %copy-start.3 = (bf16[1,512,128]{2,1,0:T(8,128)(2,1)S(1)}, bf16[1,512,128]{2,1,0:T(8,128)(2,1)}, u32[]{:S(2)}) copy-start(bf16[1,512,128]{2,1,0:T(8,128)(2,1)} %param.14) | copy-start | bytes 393220
  35.4 6.8 %copy-start.1 = (bf16[128,8,512]{2,0,1:T(8,128)(2,1)}, bf16[128,8,512]{2,0,1:T(8,128)(2,1)S(1)}, u32[]{:S(2)}) copy-start(bf16[128,8,512]{2,0,1:T(8,128)(2,1)S(1)} %all-to-all-done.1) | copy-start | bytes 3145732
  35.4 29.5 %all-to-all-start.2 = ((bf16[128,8,512]{2,0,1:T(8,128)(2,1)}), bf16[128,8,512]{2,0,1:T(8,128)(2,1)S(1)}, u32[]{:S(2)}, u32[]{:S(2)}) async-start(bf16[128,8,512]{2,0,1:T(8,128)(2,1)} %bitcast.70), calls=%async_computation.2 | async-start | bytes 2097152 | tf_op jit(solution)/shard_map/all_to_all | solution.py:71
  39.0 3.2 copy-start.7
  39.0 3.2 copy-start.6
  39.0 3.2 copy-start.5
  64.9 210.7 %all-to-all-start = ((bf16[128,8,512]{2,0,1:T(8,128)(2,1)}), bf16[128,8,512]{2,0,1:T(8,128)(2,1)}, u32[]{:S(2)}, u32[]{:S(2)}) async-start(bf16[128,8,512]{2,0,1:T(8,128)(2,1)} %bitcast.72), calls=%async_computation | async-start | bytes 2097152 | tf_op jit(solution)/shard_map/all_to_all | solution.py:69
  70.9 1.2 copy-start.4
  98.1 3.4 %slice-start = ((bf16[128,32896]{0,1:T(8,128)(2,1)}), bf16[128,32768]{0,1:T(8,128)(2,1)S(1)}, s32[]{:S(2)}) async-start(bf16[128,32896]{0,1:T(8,128)(2,1)} %tile.14), calls=%async_computation.4 | async-start | bytes 16777216 | tf_op jit(solution)/shard_map/while/body/eval_jaxpr/slice | solution.py:40
  145.9 3.4 %slice-start = ((bf16[128,32896]{0,1:T(8,128)(2,1)}), bf16[128,32768]{0,1:T(8,128)(2,1)S(1)}, s32[]{:S(2)}) async-start(bf16[128,32896]{0,1:T(8,128)(2,1)} %tile.14), calls=%async_computation.4 | async-start | bytes 16777216 | tf_op jit(solution)/shard_map/while/body/eval_jaxpr/slice | solution.py:40
  193.6 3.4 %slice-start = ((bf16[128,32896]{0,1:T(8,128)(2,1)}), bf16[128,32768]{0,1:T(8,128)(2,1)S(1)}, s32[]{:S(2)}) async-start(bf16[128,32896]{0,1:T(8,128)(2,1)} %tile.14), calls=%async_computation.4 | async-start | bytes 16777216 | tf_op jit(solution)/shard_map/while/body/eval_jaxpr/slice | solution.py:40
  241.3 3.4 %slice-start = ((bf16[128,32896]{0,1:T(8,128)(2,1)}), bf16[128,32768]{0,1:T(8,128)(2,1)S(1)}, s32[]{:S(2)}) async-start(bf16[128,32896]{0,1:T(8,128)(2,1)} %tile.14), calls=%async_computation.4 | async-start | bytes 16777216 | tf_op jit(solution)/shard_map/while/body/eval_jaxpr/slice | solution.py:40
  275.6 1.9 copy-start
  309.7 14.3 %collective-permute-start = (bf16[128,4096]{0,1:T(8,128)(2,1)S(1)}, bf16[128,4096]{0,1:T(8,128)(2,1)S(1)}, u32[]{:S(2)}, u32[]{:S(2)}) collective-permute-start(bf16[128,4096]{0,1:T(8,128)(2,1)S(1)} %bitcast.100), channel_id=1, source_target_pairs={{0,8},{8,16},{16,24},{24,0},{1,9},{9,17},{17,25},{25,1},{2,10},{10... | collective-permute-start | bytes 3145736 | tf_op jit(solution)/shard_map/ppermute | solution.py:10
where the time goes:
time: 328 us; the launch traced here: 325 us
  local copies, waits for them, and re-layouts  174 us (53%)
  waiting for transfers between devices  60 us (18%)
  matrix products  39.1 us (12%)
  blocking collectives  30.6 us (9%)
  starting transfers between devices  15.1 us (5%)
  other arithmetic  6 us (2%)
    another operation x12, local copies, waits for them, and re-layouts, one_group(): tiled = jnp.tile(group_taps, (1, 128))[:, :128 * 256]  69.5 us
    while x8, local copies, waits for them, and re-layouts  53.7 us
    all_to_all x1, blocking collectives, body(): lax.all_to_all(mixed, 'ctx', split_axis=0, concat_axis=1, tiled=True)  30.6 us
    all_to_all x1, waiting for transfers between devices, body(): lax.all_to_all(key_rows, 'ctx', split_axis=1, concat_axis=0, tiled=True)  24.6 us
    dot_general x4, matrix products, one_group(): jnp.einsum('cij,bjc->bic', toeplitz[:, :, 128:], upper_part, preferred_el...  21.4 us
    all_to_all x1, waiting for transfers between devices, body(): lax.all_to_all(value_rows, 'ctx', split_axis=1, concat_axis=0, tiled=True)  21.1 us
    dot_general x4, matrix products, one_group(): jnp.einsum('cij,bjc->bic', toeplitz[:, :, :128], lower_part, preferred_el...  17.7 us
    slice x4, local copies, waits for them, and re-layouts, one_group(): toeplitz[:, :, 128:]  15.1 us
  transfers between devices with their start and end apart: 4, of which 3 were waited for; matrix products, arithmetic and copies ran while one was open for 61% of the time, Pallas kernels for 0%

commit v1 on v0

v1 whole, which is shorter than its diff:
```python
import functools

import jax
import jax.numpy as jnp
import numpy as np
from jax import lax
from jax.experimental import pallas as pl
from jax.experimental.pallas import tpu as pltpu
from jax.sharding import PartitionSpec as P

MESH = pl.DeviceIdType.MESH
F32 = jnp.float32
BF16 = jnp.bfloat16


def transforms(block):
    size = 2 * block
    freq = (2 * np.arange(block)[:, None] + 1).astype(np.int64)
    turn = np.pi * ((freq * np.arange(size)[None, :]) % (2 * size)) / size
    forward = np.concatenate([np.cos(turn), -np.sin(turn)], axis=0)
    inverse = (forward * (2.0 / size)).T[block:]

    def two_terms(matrix):
        high = matrix.astype(jnp.bfloat16)
        low = (matrix - high.astype(np.float64)).astype(jnp.bfloat16)
        return np.stack([high, low])

    return two_terms(forward), two_terms(inverse)


def dot(a, b):
    return jnp.dot(a, b, preferred_element_type=F32)


def kernel(
    n_section, n_ctx,
    q_hbm, k_hbm, v_hbm, short_ref, taps_ref, gain_ref, prior_ref, tail_ref, fwd_ref, inv_ref,
    out_ref,
    q_ref, k_ref, v_ref, own_msg, msgs, taps_all, own_tail, edge_out, edge_in, edges,
    p_out, p_own, p_in, hist, prev, f_out, f_in, mixed,
    load_sem, msg_send, msg_recv, taps_send, taps_recv, tail_send, hist_send, hist_recv,
    edge_send, edge_recv, p_send, p_recv, f_send, f_recv, out_send, out_recv,
):
    section = lax.axis_index("section")
    me = lax.axis_index("ctx")
    rows_of = n_ctx // 2
    z, x = me // 2, me % 2
    partner = me + 1 - 2 * x
    after = lax.rem(section + 1, n_section)
    before = lax.rem(section + n_section - 1, n_section)
    block, channels = q_ref.shape
    width = channels // n_ctx
    half = channels // 2

    loads = [
        pltpu.make_async_copy(src, dst, load_sem.at[i])
        for i, (src, dst) in enumerate(((q_hbm, q_ref), (k_hbm, k_ref), (v_hbm, v_ref)))
    ]
    for load in loads:
        load.start()

    barrier = pltpu.get_barrier_semaphore()
    for step in range(1, n_ctx):
        pl.semaphore_signal(
            barrier, inc=1, device_id={"ctx": lax.rem(me + step, n_ctx)}, device_id_type=MESH
        )
    for other in (after, before):
        pl.semaphore_signal(barrier, inc=1, device_id={"section": other}, device_id_type=MESH)

    pieces = [short_ref[0, m].astype(F32) for m in range(3)]
    pieces += [prior_ref[0, m].astype(F32) for m in range(3)]
    pieces.append(gain_ref[...].astype(F32))
    own_msg[...] = jnp.concatenate(pieces, axis=0).astype(BF16)
    msgs[me] = own_msg[...]
    own_tail[...] = jnp.concatenate(
        [jnp.zeros((1, width), F32), tail_ref[0].astype(F32)], axis=0
    ).astype(BF16)
    taps_all[z] = taps_ref[0]

    @pl.when(z == 0)
    def _():
        hist[0] = own_tail[...]

    for load in loads:
        load.wait()
    last = [ref[block - 16:, :].astype(F32)[14:] for ref in (q_ref, k_ref, v_ref)]
    edge_out[...] = jnp.concatenate(
        [piece[:, :half] for piece in last]
        + [piece[:, half:] for piece in last]
        + [jnp.zeros((4, half), F32)],
        axis=0,
    ).astype(BF16)

    pl.semaphore_wait(barrier, n_ctx + 1)

    def remote(src, dst, send, recv, **where):
        return pltpu.make_async_remote_copy(
            src_ref=src, dst_ref=dst, send_sem=send, recv_sem=recv,
            device_id=where, device_id_type=MESH,
        )

    def edge_copy():
        return remote(edge_out, edge_in, edge_send, edge_recv, ctx=lax.rem(me + 1, n_ctx))

    def msg_copy(step, slot):
        return remote(
            own_msg, msgs.at[slot], msg_send.at[step], msg_recv.at[step],
            ctx=lax.rem(me + step, n_ctx),
        )

    def taps_copy(step, slot):
        return remote(
            taps_ref.at[0], taps_all.at[slot], taps_send.at[step], taps_recv.at[step],
            ctx=lax.rem(z + step, rows_of) * 2 + x,
        )

    def tail_copy():
        return remote(own_tail, hist.at[z], tail_send, hist_recv.at[z], ctx=x)

    def hist_copy(src, i):
        return remote(
            src.at[i], hist.at[i], hist_send.at[i], hist_recv.at[i],
            ctx=lax.rem(me + 2, n_ctx),
        )

    def p_copy(i):
        return remote(p_out.at[i], p_in.at[i], p_send.at[i], p_recv.at[i], ctx=partner)

    def f_copy(i):
        return remote(f_out.at[i], f_in.at[i], f_send.at[i], f_recv.at[i], ctx=partner)

    def columns(c):
        return pl.ds(pl.multiple_of(c * width, 128), width)

    def out_copy(c):
        return remote(
            mixed.at[:, columns(c)], out_ref.at[:, columns(c)], out_send.at[c], out_recv.at[c],
            section=after,
        )

    @pl.when(me < n_ctx - 1)
    def _():
        edge_copy().start()

    for step in range(1, n_ctx):
        msg_copy(step, me).start()
    for step in range(1, rows_of):
        taps_copy(step, z).start()

    @pl.when(z > 0)
    def _():
        tail_copy().start()

    for step in range(1, n_ctx):
        msg_copy(step, lax.rem(me - step + n_ctx, n_ctx)).wait_recv()

    @pl.when(me > 0)
    def _():
        edge_copy().wait_recv()
        got = edge_in[...].astype(F32)
        edges[0:6, :half] = got[0:6]
        edges[0:6, half:] = got[6:12]

    @pl.when(me == 0)
    def _():
        def place(c, carry):
            edges[0:6, columns(c)] = msgs[c].astype(F32)[9:15]
            return carry

        lax.fori_loop(0, n_ctx, place, 0)

    def feature(ref, c, lane, m, message):
        at = pl.ds(pl.multiple_of(c * width + lane, 128), 128)
        rows = ref[:, at].astype(F32)
        ends = edges[:, at]
        older, newer = ends[2 * m : 2 * m + 1], ends[2 * m + 1 : 2 * m + 2]
        place = lax.broadcasted_iota(jnp.int32, rows.shape, 0)
        one = jnp.where(place == 0, newer, pltpu.roll(rows, 1, 0))
        two = jnp.where(
            place == 0, older, jnp.where(place == 1, newer, pltpu.roll(rows, 2, 0))
        )
        weights = message[3 * m : 3 * m + 3, lane : lane + 128]
        return weights[0:1] * rows + weights[1:2] * one + weights[2:3] * two

    def product(c, dst, i):
        message = msgs[c].astype(F32)
        for lane in range(0, width, 128):
            key = feature(k_ref, c, lane, 1, message)
            value = feature(v_ref, c, lane, 2, message)
            dst[i, :, lane : lane + 128] = (key * value).astype(BF16)

    def partner_products(i, carry):
        product(2 * i + 1 - x, p_out, i)
        p_copy(i).start()
        return carry

    lax.fori_loop(0, rows_of, partner_products, 0)

    def own_products(i, carry):
        product(2 * i + x, p_own, i)

        @pl.when((x == 1) & (z < rows_of - 1))
        def _():
            hist_copy(p_own, i).start()

        return carry

    lax.fori_loop(0, rows_of, own_products, 0)

    def finish(c, filtered):
        message = msgs[c].astype(F32)
        for lane in range(0, width, 128):
            at = pl.ds(pl.multiple_of(c * width + lane, 128), 128)
            query = feature(q_ref, c, lane, 0, message)
            mixed[:, at] = (query * filtered[:, lane : lane + 128]).astype(BF16)
        out_copy(c).start()

    def from_partner(i):
        f_copy(i).wait_recv()
        finish(2 * i + 1 - x, f_in[i].astype(F32))

    def spectrum(window):
        return dot(fwd_ref[0], window) + dot(fwd_ref[1], window)

    def filtered_block(current, real, imag):
        window = spectrum(jnp.concatenate([prev[...], current], axis=0))
        one, two = window[:block], window[block:]
        result = jnp.concatenate([one * real - two * imag, one * imag + two * real], axis=0)
        high = result.astype(BF16)
        low = (result - high.astype(F32)).astype(BF16)
        return dot(inv_ref[0], high) + (dot(inv_ref[1], high) + dot(inv_ref[0], low))

    def wait_hist(i):
        @pl.when((z > 0) | (i > 0))
        def _():
            hist_copy(p_own, i).wait_recv()

    def main(i, carry):
        @pl.when(i != z)
        def _():
            step = lax.rem(z - i + rows_of, rows_of)
            taps_copy(step, i).wait_recv()

        taps = taps_all[i]
        over = (((1,), (1,)), ((), ()))
        response = lax.dot_general(
            fwd_ref[0, :, :block], taps, over, preferred_element_type=F32
        ) + lax.dot_general(fwd_ref[1, :, :block], taps, over, preferred_element_type=F32)
        gain = msgs[2 * i + x].astype(F32)[15:16]
        real, imag = response[:block] + gain, response[block:]

        p_copy(i).wait_recv()

        @pl.when((x == 0) & (z < rows_of - 1))
        def _():
            hist_copy(p_in, i).start()

        @pl.when(x == 0)
        def _():
            prev[...] = p_own[i]

        @pl.when(x == 1)
        def _():
            wait_hist(i)
            prev[...] = hist[i]

        f_out[i] = filtered_block(p_in[i], real, imag).astype(BF16)
        f_copy(i).start()

        @pl.when(x == 0)
        def _():
            wait_hist(i)
            prev[...] = hist[i]

        @pl.when(x == 1)
        def _():
            prev[...] = p_in[i]

        finish(2 * i + x, filtered_block(p_own[i], real, imag))

        @pl.when(i > 0)
        def _():
            from_partner(i - 1)

        return carry

    lax.fori_loop(0, rows_of, main, 0)
    from_partner(rows_of - 1)

    @pl.when(me < n_ctx - 1)
    def _():
        edge_copy().wait_send()

    for step in range(1, n_ctx):
        msg_copy(step, me).wait_send()
    for step in range(1, rows_of):
        taps_copy(step, z).wait_send()

    @pl.when(z > 0)
    def _():
        tail_copy().wait_send()

    def drain(i, carry):
        p_copy(i).wait_send()
        f_copy(i).wait_send()

        @pl.when(z < rows_of - 1)
        def _():
            hist_copy(p_own, i).wait_send()

        return carry

    lax.fori_loop(0, rows_of, drain, 0)

    def drain_out(c, carry):
        out_copy(c).wait()
        return carry

    lax.fori_loop(0, n_ctx, drain_out, 0)


def body(n_section, n_ctx, query, key, value, short_taps, long_taps, skip_gain, prior_qkv, prior_product):
    block, channels = query.shape
    width = channels // n_ctx
    rows_of = n_ctx // 2
    forward, inverse = transforms(block)
    hbm = pl.BlockSpec(memory_space=pl.ANY)
    vmem = pl.BlockSpec(memory_space=pltpu.VMEM)
    slots = (rows_of, block, width)
    sems = pltpu.SemaphoreType.DMA
    return pl.pallas_call(
        functools.partial(kernel, n_section, n_ctx),
        out_shape=jax.ShapeDtypeStruct(query.shape, BF16),
        in_specs=[hbm] * 3 + [vmem] * 7,
        out_specs=hbm,
        scratch_shapes=[
            pltpu.VMEM((block, channels), BF16),
            pltpu.VMEM((block, channels), BF16),
            pltpu.VMEM((block, channels), BF16),
            pltpu.VMEM((16, width), BF16),
            pltpu.VMEM((n_ctx, 16, width), BF16),
            pltpu.VMEM((rows_of, width, block), BF16),
            pltpu.VMEM((block, width), BF16),
            pltpu.VMEM((16, channels // 2), BF16),
            pltpu.VMEM((16, channels // 2), BF16),
            pltpu.VMEM((8, channels), F32),
            pltpu.VMEM(slots, BF16),
            pltpu.VMEM(slots, BF16),
            pltpu.VMEM(slots, BF16),
            pltpu.VMEM(slots, BF16),
            pltpu.VMEM((block, width), BF16),
            pltpu.VMEM(slots, BF16),
            pltpu.VMEM(slots, BF16),
            pltpu.VMEM((block, channels), BF16),
            sems((3,)),
            sems((n_ctx,)),
            sems((n_ctx,)),
            sems((rows_of,)),
            sems((rows_of,)),
            sems,
            sems((rows_of,)),
            sems((rows_of,)),
            sems,
            sems,
            sems((rows_of,)),
            sems((rows_of,)),
            sems((rows_of,)),
            sems((rows_of,)),
            sems((n_ctx,)),
            sems((n_ctx,)),
        ],
        compiler_params=pltpu.CompilerParams(
            collective_id=0, has_side_effects=True, vmem_limit_bytes=40 * 1024 * 1024
        ),
        cost_estimate=pl.CostEstimate(
            flops=2 * 2 * 256 * 256 * 4096, bytes_accessed=6 * 2**20, transcendentals=0
        ),
        name="paired_filter",
    )(
        query, key, value, short_taps, long_taps, skip_gain, prior_qkv, prior_product,
        jnp.asarray(forward), jnp.asarray(inverse),
    )


def solution(mesh):
    in_specs = (
        P(("section", "ctx"), None),
        P(("section", "ctx"), None),
        P(("section", "ctx"), None),
        P("section", None, None, "ctx"),
        P("section", "ctx", None),
        P("section", "ctx"),
        P("section", None, None, "ctx"),
        P("section", None, "ctx"),
    )
    out_specs = P(("section", "ctx"), None)
    run = functools.partial(body, mesh.shape["section"], mesh.shape["ctx"])
    return jax.shard_map(run, mesh=mesh, in_specs=in_specs, out_specs=out_specs, check_vma=False)
```

time: 328 us -> 53.3 us (0.16)
  the two profiles are of different devices: /device:TPU:0 before, /device:TPU:24 now
where the time goes in v1:
time: 53.3 us; the launch traced here: 52.9 us
  Pallas kernels  42.5 us (80%)
  local copies, waits for them, and re-layouts  10.4 us (20%)
    pallas_call x1, Pallas kernels, body(): pl.pallas_call(functools.partial(kernel, n_section, n_ctx), out_shape=jax...  42.5 us
    unnamed x21, local copies, waits for them, and re-layouts  10.4 us

profile of v1, /device:TPU:24, one launch (start us, length us, event | category | flops | bytes accessed | tf_op | source)
XLA Modules:
  0.0 52.9 jit_solution(15224674477970927792)
XLA Ops:
  0.0 0.0 copy-start
  0.0 1.2 %copy-done = bf16[128,4096]{1,0:T(8,128)(2,1)S(1)} copy-done((bf16[128,4096]{1,0:T(8,128)(2,1)S(1)}, bf16[128,4096]{1,0:T(8,128)(2,1)}, u32[]{:S(2)}) %copy-start) | copy-done | bytes 1048600
  1.2 0.0 copy-start.1
  1.2 1.2 %copy-done.1 = bf16[128,4096]{1,0:T(8,128)(2,1)S(1)} copy-done((bf16[128,4096]{1,0:T(8,128)(2,1)S(1)}, bf16[128,4096]{1,0:T(8,128)(2,1)}, u32[]{:S(2)}) %copy-start.1) | copy-done | bytes 1048600
  2.5 0.0 copy-start.2
  2.5 1.2 %copy-done.2 = bf16[128,4096]{1,0:T(8,128)(2,1)S(1)} copy-done((bf16[128,4096]{1,0:T(8,128)(2,1)S(1)}, bf16[128,4096]{1,0:T(8,128)(2,1)}, u32[]{:S(2)}) %copy-start.2) | copy-done | bytes 1048600
  3.7 0.0 copy-start.3
  3.7 0.9 %copy-done.3 = bf16[2,256,256]{2,1,0:T(8,128)(2,1)S(1)} copy-done((bf16[2,256,256]{2,1,0:T(8,128)(2,1)S(1)}, bf16[2,256,256]{2,1,0:T(8,128)(2,1)}, u32[]{:S(2)}) %copy-start.3) | copy-done | bytes 262168
  4.6 0.0 copy-start.4
  4.6 0.9 %copy-done.4 = bf16[1,512,128]{2,1,0:T(8,128)(2,1)S(1)} copy-done((bf16[1,512,128]{2,1,0:T(8,128)(2,1)S(1)}, bf16[1,512,128]{2,1,0:T(8,128)(2,1)}, u32[]{:S(2)}) %copy-start.4) | copy-done | bytes 131096
  5.5 0.0 copy-start.5
  5.5 0.9 %copy-done.5 = bf16[1,127,512]{2,1,0:T(8,128)(2,1)S(1)} copy-done((bf16[1,127,512]{2,1,0:T(8,128)(2,1)S(1)}, bf16[1,127,512]{2,1,0:T(8,128)(2,1)}, u32[]{:S(2)}) %copy-start.5) | copy-done | bytes 130072
  6.4 0.0 copy-start.6
  6.4 0.9 %copy-done.6 = bf16[2,128,256]{2,1,0:T(8,128)(2,1)S(1)} copy-done((bf16[2,128,256]{2,1,0:T(8,128)(2,1)S(1)}, bf16[2,128,256]{2,1,0:T(8,128)(2,1)}, u32[]{:S(2)}) %copy-start.6) | copy-done | bytes 131096
  7.3 0.0 copy-start.7
  7.3 0.7 %copy-done.7 = bf16[1,3,3,512]{3,2,1,0:T(4,128)(2,1)S(1)} copy-done((bf16[1,3,3,512]{3,2,1,0:T(4,128)(2,1)S(1)}, bf16[1,3,3,512]{3,2,1,0:T(4,128)(2,1)}, u32[]{:S(2)}) %copy-start.7) | copy-done | bytes 9240
  8.0 0.0 copy-start.8
  8.1 0.7 %copy-done.8 = bf16[1,3,2,512]{3,2,1,0:T(2,128)(2,1)S(1)} copy-done((bf16[1,3,2,512]{3,2,1,0:T(2,128)(2,1)S(1)}, bf16[1,3,2,512]{3,2,1,0:T(2,128)(2,1)}, u32[]{:S(2)}) %copy-start.8) | copy-done | bytes 6168
  8.7 0.0 copy-start.9
  8.7 0.7 %copy-done.9 = bf16[1,512]{1,0:T(2,128)(2,1)S(1)} copy-done((bf16[1,512]{1,0:T(2,128)(2,1)S(1)}, bf16[1,512]{1,0:T(2,128)(2,1)}, u32[]{:S(2)}) %copy-start.9) | copy-done | bytes 1048
  9.4 42.5 %paired_filter.1 = bf16[128,4096]{1,0:T(8,128)(2,1)S(1)} custom-call(bf16[128,4096]{1,0:T(8,128)(2,1)S(1)} %copy-done, bf16[128,4096]{1,0:T(8,128)(2,1)S(1)} %copy-done.1, bf16[128,4096]{1,0:T(8,128)(2,1)S(1)} %copy-done.2, bf16[1,3,3,512]{3,2,1,0:T(4,128)(2,1)S(1)} %copy-done.7, bf16[1,512,128]{2,1,0:T(8,128)(2,1)S(1)} %copy-done.4, ...), custom_call_target="tpu_custom_call" | custom-call | flops 1073741824 | bytes 6291456 | tf_op jit(solution)/shard_map/paired_filter/pallas_call | solution.py:331
  51.9 1.0 %copy.12 = bf16[128,4096]{1,0:T(8,128)(2,1)} copy(bf16[128,4096]{1,0:T(8,128)(2,1)S(1)} %paired_filter.1) | data formatting | bytes 2097152
Async XLA Ops:
  0.0 1.2 %copy-start = (bf16[128,4096]{1,0:T(8,128)(2,1)S(1)}, bf16[128,4096]{1,0:T(8,128)(2,1)}, u32[]{:S(2)}) copy-start(bf16[128,4096]{1,0:T(8,128)(2,1)} %q_hbm.1) | copy-start | bytes 3145732
  1.2 1.2 %copy-start.1 = (bf16[128,4096]{1,0:T(8,128)(2,1)S(1)}, bf16[128,4096]{1,0:T(8,128)(2,1)}, u32[]{:S(2)}) copy-start(bf16[128,4096]{1,0:T(8,128)(2,1)} %k_hbm.1) | copy-start | bytes 3145732
  2.5 1.2 %copy-start.2 = (bf16[128,4096]{1,0:T(8,128)(2,1)S(1)}, bf16[128,4096]{1,0:T(8,128)(2,1)}, u32[]{:S(2)}) copy-start(bf16[128,4096]{1,0:T(8,128)(2,1)} %v_hbm.1) | copy-start | bytes 3145732
  3.7 0.9 %copy-start.3 = (bf16[2,256,256]{2,1,0:T(8,128)(2,1)S(1)}, bf16[2,256,256]{2,1,0:T(8,128)(2,1)}, u32[]{:S(2)}) copy-start(bf16[2,256,256]{2,1,0:T(8,128)(2,1)} %constant.4.clone.fwd_ref) | copy-start | bytes 786436
  4.6 0.9 %copy-start.4 = (bf16[1,512,128]{2,1,0:T(8,128)(2,1)S(1)}, bf16[1,512,128]{2,1,0:T(8,128)(2,1)}, u32[]{:S(2)}) copy-start(bf16[1,512,128]{2,1,0:T(8,128)(2,1)} %taps_ref.1) | copy-start | bytes 393220
  5.5 0.9 %copy-start.5 = (bf16[1,127,512]{2,1,0:T(8,128)(2,1)S(1)}, bf16[1,127,512]{2,1,0:T(8,128)(2,1)}, u32[]{:S(2)}) copy-start(bf16[1,127,512]{2,1,0:T(8,128)(2,1)} %tail_ref.1) | copy-start | bytes 390148
  6.4 0.9 %copy-start.6 = (bf16[2,128,256]{2,1,0:T(8,128)(2,1)S(1)}, bf16[2,128,256]{2,1,0:T(8,128)(2,1)}, u32[]{:S(2)}) copy-start(bf16[2,128,256]{2,1,0:T(8,128)(2,1)} %constant.5.clone.inv_ref) | copy-start | bytes 393220
  7.3 0.7 %copy-start.7 = (bf16[1,3,3,512]{3,2,1,0:T(4,128)(2,1)S(1)}, bf16[1,3,3,512]{3,2,1,0:T(4,128)(2,1)}, u32[]{:S(2)}) copy-start(bf16[1,3,3,512]{3,2,1,0:T(4,128)(2,1)} %short_ref.1) | copy-start | bytes 27652
  8.0 0.7 %copy-start.8 = (bf16[1,3,2,512]{3,2,1,0:T(2,128)(2,1)S(1)}, bf16[1,3,2,512]{3,2,1,0:T(2,128)(2,1)}, u32[]{:S(2)}) copy-start(bf16[1,3,2,512]{3,2,1,0:T(2,128)(2,1)} %prior_ref.1) | copy-start | bytes 18436
  8.7 0.7 %copy-start.9 = (bf16[1,512]{1,0:T(2,128)(2,1)S(1)}, bf16[1,512]{1,0:T(2,128)(2,1)}, u32[]{:S(2)}) copy-start(bf16[1,512]{1,0:T(2,128)(2,1)} %gain_ref.1) | copy-start | bytes 3076

commit v2 on v1

v2 whole, which is shorter than its diff:
```python
import functools

import jax
import jax.numpy as jnp
import numpy as np
from jax import lax
from jax.experimental import pallas as pl
from jax.experimental.pallas import tpu as pltpu
from jax.sharding import PartitionSpec as P

MESH = pl.DeviceIdType.MESH
F32 = jnp.float32
BF16 = jnp.bfloat16
CHUNK = 512
VMEM_BYTES = 64 * 1024 * 1024


def transforms(block):
    size = 2 * block
    freq = (2 * np.arange(block)[:, None] + 1).astype(np.int64)
    turn = np.pi * ((freq * np.arange(size)[None, :]) % (2 * size)) / size
    forward = np.concatenate([np.cos(turn), -np.sin(turn)], axis=0)
    inverse = (forward * (2.0 / size)).T[block:]

    return forward.astype(np.float32), inverse.astype(np.float32)


def two_terms(matrix):
    high = matrix.astype(BF16)
    return high, (matrix - high.astype(F32)).astype(BF16)


def dot(a, b):
    return jnp.dot(a, b, preferred_element_type=F32)


def kernel(
    n_section, n_ctx,
    q_hbm, k_hbm, v_hbm, short_hbm, taps_hbm, gain_hbm, prior_hbm, tail_hbm, fwd_hbm, inv_hbm,
    out_ref,
    q_ref, k_ref, v_ref, short_ref, gain_ref, prior_ref, tail_ref, fwd_f32, inv_f32, fwd_ref, inv_ref, own_msg, msgs, taps_all, own_tail, edge_out, edge_in, edges,
    p_out, p_own, p_in, hist, prev, f_out, f_in, mixed,
    load_sem, msg_send, msg_recv, taps_send, taps_recv, tail_send, hist_send, hist_recv,
    edge_send, edge_recv, p_send, p_recv, f_send, f_recv, out_send, out_recv,
):
    section = lax.axis_index("section")
    me = lax.axis_index("ctx")
    rows_of = n_ctx // 2
    z, x = me // 2, me % 2
    partner = me + 1 - 2 * x
    after = lax.rem(section + 1, n_section)
    before = lax.rem(section + n_section - 1, n_section)
    block, channels = q_ref.shape
    width = channels // n_ctx
    half = channels // 2

    sub = p_out.shape[2]
    parts = width // sub

    loads = [
        pltpu.make_async_copy(src, dst, load_sem.at[i])
        for i, (src, dst) in enumerate(
            (
                (short_hbm, short_ref), (prior_hbm, prior_ref), (gain_hbm, gain_ref),
                (tail_hbm, tail_ref), (k_hbm, k_ref), (v_hbm, v_ref), (q_hbm, q_ref),
                (taps_hbm.at[0], taps_all.at[z]), (fwd_hbm, fwd_f32), (inv_hbm, inv_f32),
            )
        )
    ]
    for load in loads:
        load.start()

    barrier = pltpu.get_barrier_semaphore()
    for step in range(1, n_ctx):
        pl.semaphore_signal(
            barrier, inc=1, device_id={"ctx": lax.rem(me + step, n_ctx)}, device_id_type=MESH
        )
    for other in (after, before):
        pl.semaphore_signal(barrier, inc=1, device_id={"section": other}, device_id_type=MESH)

    for load in loads[:4]:
        load.wait()
    pieces = [short_ref[0, m].astype(F32) for m in range(3)]
    pieces += [prior_ref[0, m].astype(F32) for m in range(3)]
    pieces.append(gain_ref[...].astype(F32))
    own_msg[...] = jnp.concatenate(pieces, axis=0).astype(BF16)
    msgs[me] = own_msg[...]
    tail = jnp.concatenate(
        [jnp.zeros((1, width), F32), tail_ref[0].astype(F32)], axis=0
    ).astype(BF16)
    for part in range(parts):
        own_tail[part] = tail[:, part * sub : (part + 1) * sub]

    @pl.when(z == 0)
    def _():
        for part in range(parts):
            hist[part] = own_tail[part]

    for load in loads[4:7]:
        load.wait()
    last = [ref[block - 16:, :].astype(F32)[14:] for ref in (q_ref, k_ref, v_ref)]
    edge_out[...] = jnp.concatenate(
        [piece[:, :half] for piece in last]
        + [piece[:, half:] for piece in last]
        + [jnp.zeros((4, half), F32)],
        axis=0,
    ).astype(BF16)

    pl.semaphore_wait(barrier, n_ctx + 1)

    def remote(src, dst, send, recv, **where):
        return pltpu.make_async_remote_copy(
            src_ref=src, dst_ref=dst, send_sem=send, recv_sem=recv,
            device_id=where, device_id_type=MESH,
        )

    chunks = rows_of * parts
    partner_step = lax.rem(partner - me + n_ctx, n_ctx)

    def edge_copy():
        return remote(edge_out, edge_in, edge_send, edge_recv, ctx=lax.rem(me + 1, n_ctx))

    def msg_copy(step, slot):
        return remote(
            own_msg, msgs.at[slot], msg_send.at[step], msg_recv.at[step],
            ctx=lax.rem(me + step, n_ctx),
        )

    def taps_copy(step, slot):
        return remote(
            taps_hbm.at[0], taps_all.at[slot], taps_send.at[step], taps_recv.at[step],
            ctx=lax.rem(z + step, rows_of) * 2 + x,
        )

    def tail_copy(part):
        slot = z * parts + part
        return remote(
            own_tail.at[part], hist.at[slot], tail_send.at[part], hist_recv.at[slot], ctx=x
        )

    def hist_copy(src, i):
        return remote(
            src.at[i], hist.at[i], hist_send.at[i], hist_recv.at[i],
            ctx=lax.rem(me + 2, n_ctx),
        )

    def p_copy(i):
        return remote(p_out.at[i], p_in.at[i], p_send.at[i], p_recv.at[i], ctx=partner)

    def f_copy(i):
        return remote(f_out.at[i], f_in.at[i], f_send.at[i], f_recv.at[i], ctx=partner)

    def columns(c):
        return pl.ds(pl.multiple_of(c * width, 128), width)

    def out_copy(t):
        at = pl.ds(pl.multiple_of(t * sub, 128), sub)
        return remote(
            mixed.at[:, at], out_ref.at[:, at], out_send.at[t], out_recv.at[t], section=after
        )

    def chunk(n):
        row = lax.rem(z + n // parts, rows_of)
        part = lax.rem(n, parts)
        return row * parts + part, row, part

    @pl.when(me < n_ctx - 1)
    def _():
        edge_copy().start()

    msg_copy(partner_step, me).start()
    for step in range(n_ctx - 1, 0, -1):

        @pl.when(step != partner_step)
        def _():
            msg_copy(step, me).start()

    for step in range(rows_of - 1, 0, -1):
        taps_copy(step, z).start()

    @pl.when(z > 0)
    def _():
        for part in range(parts):
            tail_copy(part).start()

    def wait_msg(c):
        @pl.when(c != me)
        def _():
            msg_copy(lax.rem(me - c + n_ctx, n_ctx), c).wait_recv()

    @pl.when(me > 0)
    def _():
        edge_copy().wait_recv()
        got = edge_in[...].astype(F32)
        edges[0:6, :half] = got[0:6]
        edges[0:6, half:] = got[6:12]

    def place_edge(c):
        @pl.when(me == 0)
        def _():
            edges[0:6, columns(c)] = msgs[c].astype(F32)[9:15]

    def feature(ref, at, m, weights):
        rows = ref[:, at].astype(F32)
        ends = edges[0:6, at]
        older, newer = ends[2 * m : 2 * m + 1], ends[2 * m + 1 : 2 * m + 2]
        place = lax.broadcasted_iota(jnp.int32, rows.shape, 0)
        one = jnp.where(place == 0, newer, pltpu.roll(rows, 1, 0))
        two = jnp.where(
            place == 0, older, jnp.where(place == 1, newer, pltpu.roll(rows, 2, 0))
        )
        taps = weights[3 * m : 3 * m + 3]
        return taps[0:1] * rows + taps[1:2] * one + taps[2:3] * two

    def lanes(c, part):
        for lane in range(0, sub, 128):
            inside = pl.ds(pl.multiple_of(part * sub + lane, 128), 128)
            at = pl.ds(pl.multiple_of(c * width + part * sub + lane, 128), 128)
            yield lane, at, msgs[c, :, inside].astype(F32)

    def product(c, part, dst, slot):
        for lane, at, weights in lanes(c, part):
            key = feature(k_ref, at, 1, weights)
            value = feature(v_ref, at, 2, weights)
            dst[slot, :, lane : lane + 128] = (key * value).astype(BF16)

    def partner_products(n, carry):
        slot, row, part = chunk(n)
        c = 2 * row + 1 - x

        @pl.when(part == 0)
        def _():
            wait_msg(c)
            place_edge(c)

        product(c, part, p_out, slot)
        p_copy(slot).start()
        return carry

    lax.fori_loop(0, chunks, partner_products, 0)

    def own_products(n, carry):
        slot, row, part = chunk(n)
        c = 2 * row + x

        @pl.when(part == 0)
        def _():
            wait_msg(c)
            place_edge(c)

        product(c, part, p_own, slot)

        @pl.when((x == 1) & (z < rows_of - 1))
        def _():
            hist_copy(p_own, slot).start()

        return carry

    lax.fori_loop(0, chunks, own_products, 0)
    for load in loads[7:]:
        load.wait()
    fwd_ref[0], fwd_ref[1] = two_terms(fwd_f32[...])
    inv_ref[0], inv_ref[1] = two_terms(inv_f32[...])

    def finish(c, part, filtered):
        for lane, at, weights in lanes(c, part):
            query = feature(q_ref, at, 0, weights)
            mixed[:, at] = (query * filtered[:, lane : lane + 128]).astype(BF16)
        out_copy(c * parts + part).start()

    def from_partner(n):
        slot, row, part = chunk(n)
        f_copy(slot).wait_recv()
        finish(2 * row + 1 - x, part, f_in[slot].astype(F32))

    def spectrum(window):
        return dot(fwd_ref[0], window) + dot(fwd_ref[1], window)

    def filtered_block(current, real, imag):
        window = spectrum(jnp.concatenate([prev[...], current], axis=0))
        one, two = window[:block], window[block:]
        result = jnp.concatenate([one * real - two * imag, one * imag + two * real], axis=0)
        high, low = two_terms(result)
        return dot(inv_ref[0], high) + (dot(inv_ref[1], high) + dot(inv_ref[0], low))

    def wait_hist(slot):
        @pl.when((z > 0) | (slot >= parts))
        def _():
            hist_copy(p_own, slot).wait_recv()

    def main(n, carry):
        slot, row, part = chunk(n)

        @pl.when((n >= parts) & (part == 0))
        def _():
            taps_copy(lax.rem(z - row + rows_of, rows_of), row).wait_recv()

        at = pl.ds(pl.multiple_of(part * sub, 128), sub)
        taps = taps_all[row, at, :]
        over = (((1,), (1,)), ((), ()))
        response = lax.dot_general(
            fwd_ref[0, :, :block], taps, over, preferred_element_type=F32
        ) + lax.dot_general(fwd_ref[1, :, :block], taps, over, preferred_element_type=F32)
        gain = msgs[2 * row + x, :, at].astype(F32)[15:16]
        real, imag = response[:block] + gain, response[block:]

        p_copy(slot).wait_recv()

        @pl.when((x == 0) & (z < rows_of - 1))
        def _():
            hist_copy(p_in, slot).start()

        @pl.when(x == 0)
        def _():
            prev[...] = p_own[slot]

        @pl.when(x == 1)
        def _():
            wait_hist(slot)
            prev[...] = hist[slot]

        f_out[slot] = filtered_block(p_in[slot], real, imag).astype(BF16)
        f_copy(slot).start()

        @pl.when(x == 0)
        def _():
            wait_hist(slot)
            prev[...] = hist[slot]

        @pl.when(x == 1)
        def _():
            prev[...] = p_in[slot]

        finish(2 * row + x, part, filtered_block(p_own[slot], real, imag))

        @pl.when(n > 0)
        def _():
            from_partner(n - 1)

        return carry

    lax.fori_loop(0, chunks, main, 0)
    from_partner(chunks - 1)

    @pl.when(me < n_ctx - 1)
    def _():
        edge_copy().wait_send()

    for step in range(1, n_ctx):
        msg_copy(step, me).wait_send()
    for step in range(1, rows_of):
        taps_copy(step, z).wait_send()

    @pl.when(z > 0)
    def _():
        for part in range(parts):
            tail_copy(part).wait_send()

    def drain(i, carry):
        p_copy(i).wait_send()
        f_copy(i).wait_send()

        @pl.when(z < rows_of - 1)
        def _():
            hist_copy(p_own, i).wait_send()

        return carry

    lax.fori_loop(0, chunks, drain, 0)

    def drain_out(t, carry):
        out_copy(t).wait()
        return carry

    lax.fori_loop(0, 2 * chunks, drain_out, 0)


def body(n_section, n_ctx, query, key, value, short_taps, long_taps, skip_gain, prior_qkv, prior_product):
    block, channels = query.shape
    width = channels // n_ctx
    rows_of = n_ctx // 2
    forward, inverse = transforms(block)
    hbm = pl.BlockSpec(memory_space=pl.ANY)
    sub = min(width, CHUNK)
    chunks = rows_of * width // sub
    slots = (chunks, block, sub)
    sems = pltpu.SemaphoreType.DMA
    return pl.pallas_call(
        functools.partial(kernel, n_section, n_ctx),
        out_shape=jax.ShapeDtypeStruct(query.shape, BF16),
        in_specs=[hbm] * 10,
        out_specs=hbm,
        scratch_shapes=[
            pltpu.VMEM((block, channels), BF16),
            pltpu.VMEM((block, channels), BF16),
            pltpu.VMEM((block, channels), BF16),
            pltpu.VMEM(short_taps.shape, BF16),
            pltpu.VMEM(skip_gain.shape, BF16),
            pltpu.VMEM(prior_qkv.shape, BF16),
            pltpu.VMEM(prior_product.shape, BF16),
            pltpu.VMEM(forward.shape, F32),
            pltpu.VMEM(inverse.shape, F32),
            pltpu.VMEM((2,) + forward.shape, BF16),
            pltpu.VMEM((2,) + inverse.shape, BF16),
            pltpu.VMEM((16, width), BF16),
            pltpu.VMEM((n_ctx, 16, width), BF16),
            pltpu.VMEM((rows_of, width, block), BF16),
            pltpu.VMEM((width // sub, block, sub), BF16),
            pltpu.VMEM((16, channels // 2), BF16),
            pltpu.VMEM((16, channels // 2), BF16),
            pltpu.VMEM((8, channels), F32),
            pltpu.VMEM(slots, BF16),
            pltpu.VMEM(slots, BF16),
            pltpu.VMEM(slots, BF16),
            pltpu.VMEM(slots, BF16),
            pltpu.VMEM((block, sub), BF16),
            pltpu.VMEM(slots, BF16),
            pltpu.VMEM(slots, BF16),
            pltpu.VMEM((block, channels), BF16),
            sems((10,)),
            sems((n_ctx,)),
            sems((n_ctx,)),
            sems((rows_of,)),
            sems((rows_of,)),
            sems((width // sub,)),
            sems((chunks,)),
            sems((chunks,)),
            sems,
            sems,
            sems((chunks,)),
            sems((chunks,)),
            sems((chunks,)),
            sems((chunks,)),
            sems((2 * chunks,)),
            sems((2 * chunks,)),
        ],
        compiler_params=pltpu.CompilerParams(
            collective_id=0, has_side_effects=True, vmem_limit_bytes=VMEM_BYTES
        ),
        cost_estimate=pl.CostEstimate(
            flops=2 * 2 * 256 * 256 * 4096, bytes_accessed=6 * 2**20, transcendentals=0
        ),
        name="paired_filter",
    )(
        query, key, value, short_taps, long_taps, skip_gain, prior_qkv, prior_product,
        jnp.asarray(forward), jnp.asarray(inverse),
    )


def solution(mesh):
    in_specs = (
        P(("section", "ctx"), None),
        P(("section", "ctx"), None),
        P(("section", "ctx"), None),
        P("section", None, None, "ctx"),
        P("section", "ctx", None),
        P("section", "ctx"),
        P("section", None, None, "ctx"),
        P("section", None, "ctx"),
    )
    out_specs = P(("section", "ctx"), None)
    run = functools.partial(body, mesh.shape["section"], mesh.shape["ctx"])
    return jax.shard_map(run, mesh=mesh, in_specs=in_specs, out_specs=out_specs, check_vma=False)
```

time: 53.3 us -> 51 us (0.957)
  the two profiles are of different devices: /device:TPU:24 before, /device:TPU:27 now
where the time goes in v2:
time: 51 us; the launch traced here: 50.8 us
  Pallas kernels  48.5 us (95%)
  local copies, waits for them, and re-layouts  2.29 us (4%)
    pallas_call x1, Pallas kernels, body(): pl.pallas_call(functools.partial(kernel, n_section, n_ctx), out_shape=jax...  48.5 us
    unnamed x1, local copies, waits for them, and re-layouts  2.29 us

profile of v2, /device:TPU:27, one launch (start us, length us, event | category | flops | bytes accessed | tf_op | source)
XLA Modules:
  0.0 50.8 jit_solution(6601783332708456727)
XLA Ops:
  0.0 48.5 %paired_filter.1 = bf16[128,4096]{1,0:T(8,128)(2,1)} custom-call(bf16[128,4096]{1,0:T(8,128)(2,1)} %q_hbm.1, bf16[128,4096]{1,0:T(8,128)(2,1)} %k_hbm.1, bf16[128,4096]{1,0:T(8,128)(2,1)} %v_hbm.1, bf16[1,3,3,512]{3,2,1,0:T(4,128)(2,1)} %short_hbm.1, bf16[1,512,128]{2,1,0:T(8,128)(2,1)} %taps_hbm.1, bf16[1,512]{1,0:T(2,128)(2,1)} %gain_hbm.1, ...), custom_call_target="tpu_custom_call" | custom-call | flops 1073741824 | bytes 6291456 | tf_op jit(solution)/shard_map/paired_filter/pallas_call | solution.py:388
  48.5 2.3 %copy.12 = bf16[128,4096]{1,0:T(8,128)(2,1)} copy(bf16[128,4096]{1,0:T(8,128)(2,1)} %paired_filter.1) | data formatting | bytes 2097152

commit v3 on v2

--- a/solution.py
+++ b/solution.py
@@ -12,7 +12,7 @@
 F32 = jnp.float32
 BF16 = jnp.bfloat16
 CHUNK = 512
-VMEM_BYTES = 64 * 1024 * 1024
+VMEM_BYTES = 40 * 1024 * 1024
 
 
 def transforms(block):
@@ -39,7 +39,7 @@
     q_hbm, k_hbm, v_hbm, short_hbm, taps_hbm, gain_hbm, prior_hbm, tail_hbm, fwd_hbm, inv_hbm,
     out_ref,
     q_ref, k_ref, v_ref, short_ref, gain_ref, prior_ref, tail_ref, fwd_f32, inv_f32, fwd_ref, inv_ref, own_msg, msgs, taps_all, own_tail, edge_out, edge_in, edges,
-    p_out, p_own, p_in, hist, prev, f_out, f_in, mixed,
+    p_out, p_own, p_in, hist, responses, f_out, f_in, mixed,
     load_sem, msg_send, msg_recv, taps_send, taps_recv, tail_send, hist_send, hist_recv,
     edge_send, edge_recv, p_send, p_recv, f_send, f_recv, out_send, out_recv,
 ):
@@ -240,7 +240,7 @@
     lax.fori_loop(0, chunks, partner_products, 0)
 
     def own_products(n, carry):
-        slot, row, part = chunk(n)
+        slot, row, part = chunk(n + parts)
         c = 2 * row + x
 
         @pl.when(part == 0)
@@ -276,19 +276,29 @@
     def spectrum(window):
         return dot(fwd_ref[0], window) + dot(fwd_ref[1], window)
 
-    def filtered_block(current, real, imag):
-        window = spectrum(jnp.concatenate([prev[...], current], axis=0))
-        one, two = window[:block], window[block:]
+    def filtered_block(slot, before_ref, current_ref):
+        window = jnp.concatenate([before_ref[slot], current_ref[slot]], axis=0)
+        waves = spectrum(window)
+        one, two = waves[:block], waves[block:]
+        real, imag = responses[slot, :block], responses[slot, block:]
         result = jnp.concatenate([one * real - two * imag, one * imag + two * real], axis=0)
         high, low = two_terms(result)
         return dot(inv_ref[0], high) + (dot(inv_ref[1], high) + dot(inv_ref[0], low))
 
+    def give_back(slot, before_ref):
+        f_out[slot] = filtered_block(slot, before_ref, p_in).astype(BF16)
+        f_copy(slot).start()
+
+    def keep(n, before_ref):
+        slot, row, part = chunk(n)
+        finish(2 * row + x, part, filtered_block(slot, before_ref, p_own))
+
     def wait_hist(slot):
         @pl.when((z > 0) | (slot >= parts))
         def _():
             hist_copy(p_own, slot).wait_recv()
 
-    def main(n, carry):
+    def respond(n):
         slot, row, part = chunk(n)
 
         @pl.when((n >= parts) & (part == 0))
@@ -302,45 +312,50 @@
             fwd_ref[0, :, :block], taps, over, preferred_element_type=F32
         ) + lax.dot_general(fwd_ref[1, :, :block], taps, over, preferred_element_type=F32)
         gain = msgs[2 * row + x, :, at].astype(F32)[15:16]
-        real, imag = response[:block] + gain, response[block:]
-
+        responses[slot, :block] = response[:block] + gain
+        responses[slot, block:] = response[block:]
+
+    def with_product(n, carry):
+        slot, _, _ = chunk(n)
         p_copy(slot).wait_recv()
 
         @pl.when((x == 0) & (z < rows_of - 1))
         def _():
             hist_copy(p_in, slot).start()
 
+        respond(n)
+
         @pl.when(x == 0)
         def _():
-            prev[...] = p_own[slot]
+            give_back(slot, p_own)
 
         @pl.when(x == 1)
         def _():
-            wait_hist(slot)
-            prev[...] = hist[slot]
-
-        f_out[slot] = filtered_block(p_in[slot], real, imag).astype(BF16)
-        f_copy(slot).start()
+            keep(n, p_in)
+
+        return carry
+
+    def with_history(n, carry):
+        slot, _, _ = chunk(n)
+        wait_hist(slot)
 
         @pl.when(x == 0)
         def _():
-            wait_hist(slot)
-            prev[...] = hist[slot]
+            keep(n, hist)
 
         @pl.when(x == 1)
         def _():
-            prev[...] = p_in[slot]
-
-        finish(2 * row + x, part, filtered_block(p_own[slot], real, imag))
-
-        @pl.when(n > 0)
-        def _():
-            from_partner(n - 1)
-
-        return carry
-
-    lax.fori_loop(0, chunks, main, 0)
-    from_partner(chunks - 1)
+            give_back(slot, hist)
+
+        return carry
+
+    def with_partner(n, carry):
+        from_partner(n)
+        return carry
+
+    lax.fori_loop(0, chunks, with_product, 0)
+    lax.fori_loop(0, chunks, with_history, 0)
+    lax.fori_loop(0, chunks, with_partner, 0)
 
     @pl.when(me < n_ctx - 1)
     def _():
@@ -380,7 +395,7 @@
     width = channels // n_ctx
     rows_of = n_ctx // 2
     forward, inverse = transforms(block)
-    hbm = pl.BlockSpec(memory_space=pl.ANY)
+    hbm = pl.BlockSpec(memory_space=pltpu.HBM)
     sub = min(width, CHUNK)
     chunks = rows_of * width // sub
     slots = (chunks, block, sub)
@@ -389,7 +404,7 @@
         functools.partial(kernel, n_section, n_ctx),
         out_shape=jax.ShapeDtypeStruct(query.shape, BF16),
         in_specs=[hbm] * 10,
-        out_specs=hbm,
+        out_specs=pl.BlockSpec(memory_space=pl.ANY),
         scratch_shapes=[
             pltpu.VMEM((block, channels), BF16),
             pltpu.VMEM((block, channels), BF16),
@@ -413,7 +428,7 @@
             pltpu.VMEM(slots, BF16),
             pltpu.VMEM(slots, BF16),
             pltpu.VMEM(slots, BF16),
-            pltpu.VMEM((block, sub), BF16),
+            pltpu.VMEM((chunks, 2 * block, sub), F32),
             pltpu.VMEM(slots, BF16),
             pltpu.VMEM(slots, BF16),
             pltpu.VMEM((block, channels), BF16),

time: 51 us -> 52.5 us (1.029)
  the two profiles are of different devices: /device:TPU:27 before, /device:TPU:0 now
where the time goes in v3:
time: 52.5 us; the launch traced here: 52.1 us
  Pallas kernels  41.7 us (79%)
  local copies, waits for them, and re-layouts  10.4 us (20%)
    pallas_call x1, Pallas kernels, body(): pl.pallas_call(functools.partial(kernel, n_section, n_ctx), out_shape=jax...  41.7 us
    unnamed x21, local copies, waits for them, and re-layouts  10.4 us

profile of v3, /device:TPU:0, one launch (start us, length us, event | category | flops | bytes accessed | tf_op | source)
XLA Modules:
  0.0 52.1 jit_solution(1221245378700209037)
XLA Ops:
  0.0 0.0 copy-start
  0.0 1.2 %copy-done = bf16[128,4096]{1,0:T(8,128)(2,1)S(1)} copy-done((bf16[128,4096]{1,0:T(8,128)(2,1)S(1)}, bf16[128,4096]{1,0:T(8,128)(2,1)}, u32[]{:S(2)}) %copy-start) | copy-done | bytes 1048600
  1.2 0.0 copy-start.1
  1.2 1.2 %copy-done.1 = bf16[128,4096]{1,0:T(8,128)(2,1)S(1)} copy-done((bf16[128,4096]{1,0:T(8,128)(2,1)S(1)}, bf16[128,4096]{1,0:T(8,128)(2,1)}, u32[]{:S(2)}) %copy-start.1) | copy-done | bytes 1048600
  2.5 0.0 copy-start.2
  2.5 1.2 %copy-done.2 = bf16[128,4096]{1,0:T(8,128)(2,1)S(1)} copy-done((bf16[128,4096]{1,0:T(8,128)(2,1)S(1)}, bf16[128,4096]{1,0:T(8,128)(2,1)}, u32[]{:S(2)}) %copy-start.2) | copy-done | bytes 1048600
  3.7 0.0 copy-start.3
  3.7 0.9 %copy-done.3 = f32[256,256]{1,0:T(8,128)S(1)} copy-done((f32[256,256]{1,0:T(8,128)S(1)}, f32[256,256]{1,0:T(8,128)}, u32[]{:S(2)}) %copy-start.3) | copy-done | bytes 262168
  4.6 0.0 copy-start.4
  4.6 0.9 %copy-done.4 = bf16[1,512,128]{2,1,0:T(8,128)(2,1)S(1)} copy-done((bf16[1,512,128]{2,1,0:T(8,128)(2,1)S(1)}, bf16[1,512,128]{2,1,0:T(8,128)(2,1)}, u32[]{:S(2)}) %copy-start.4) | copy-done | bytes 131096
  5.5 0.0 copy-start.5
  5.5 0.9 %copy-done.5 = bf16[1,127,512]{2,1,0:T(8,128)(2,1)S(1)} copy-done((bf16[1,127,512]{2,1,0:T(8,128)(2,1)S(1)}, bf16[1,127,512]{2,1,0:T(8,128)(2,1)}, u32[]{:S(2)}) %copy-start.5) | copy-done | bytes 130072
  6.4 0.0 copy-start.6
  6.4 0.9 %copy-done.6 = f32[128,256]{1,0:T(8,128)S(1)} copy-done((f32[128,256]{1,0:T(8,128)S(1)}, f32[128,256]{1,0:T(8,128)}, u32[]{:S(2)}) %copy-start.6) | copy-done | bytes 131096
  7.3 0.0 copy-start.7
  7.3 0.7 %copy-done.7 = bf16[1,3,3,512]{3,2,1,0:T(4,128)(2,1)S(1)} copy-done((bf16[1,3,3,512]{3,2,1,0:T(4,128)(2,1)S(1)}, bf16[1,3,3,512]{3,2,1,0:T(4,128)(2,1)}, u32[]{:S(2)}) %copy-start.7) | copy-done | bytes 9240
  8.0 0.0 copy-start.8
  8.1 0.7 %copy-done.8 = bf16[1,3,2,512]{3,2,1,0:T(2,128)(2,1)S(1)} copy-done((bf16[1,3,2,512]{3,2,1,0:T(2,128)(2,1)S(1)}, bf16[1,3,2,512]{3,2,1,0:T(2,128)(2,1)}, u32[]{:S(2)}) %copy-start.8) | copy-done | bytes 6168
  8.7 0.0 copy-start.9
  8.7 0.7 %copy-done.9 = bf16[1,512]{1,0:T(2,128)(2,1)S(1)} copy-done((bf16[1,512]{1,0:T(2,128)(2,1)S(1)}, bf16[1,512]{1,0:T(2,128)(2,1)}, u32[]{:S(2)}) %copy-start.9) | copy-done | bytes 1048
  9.4 41.7 %paired_filter.1 = bf16[128,4096]{1,0:T(8,128)(2,1)S(1)} custom-call(bf16[128,4096]{1,0:T(8,128)(2,1)S(1)} %copy-done, bf16[128,4096]{1,0:T(8,128)(2,1)S(1)} %copy-done.1, bf16[128,4096]{1,0:T(8,128)(2,1)S(1)} %copy-done.2, bf16[1,3,3,512]{3,2,1,0:T(4,128)(2,1)S(1)} %copy-done.7, bf16[1,512,128]{2,1,0:T(8,128)(2,1)S(1)} %copy-done.4, ...), custom_call_target="tpu_custom_call" | custom-call | flops 1073741824 | bytes 6291456 | tf_op jit(solution)/shard_map/paired_filter/pallas_call | solution.py:403
  51.1 1.0 %copy.12 = bf16[128,4096]{1,0:T(8,128)(2,1)} copy(bf16[128,4096]{1,0:T(8,128)(2,1)S(1)} %paired_filter.1) | data formatting | bytes 2097152
Async XLA Ops:
  0.0 1.2 %copy-start = (bf16[128,4096]{1,0:T(8,128)(2,1)S(1)}, bf16[128,4096]{1,0:T(8,128)(2,1)}, u32[]{:S(2)}) copy-start(bf16[128,4096]{1,0:T(8,128)(2,1)} %q_hbm.1) | copy-start | bytes 3145732
  1.2 1.2 %copy-start.1 = (bf16[128,4096]{1,0:T(8,128)(2,1)S(1)}, bf16[128,4096]{1,0:T(8,128)(2,1)}, u32[]{:S(2)}) copy-start(bf16[128,4096]{1,0:T(8,128)(2,1)} %k_hbm.1) | copy-start | bytes 3145732
  2.5 1.2 %copy-start.2 = (bf16[128,4096]{1,0:T(8,128)(2,1)S(1)}, bf16[128,4096]{1,0:T(8,128)(2,1)}, u32[]{:S(2)}) copy-start(bf16[128,4096]{1,0:T(8,128)(2,1)} %v_hbm.1) | copy-start | bytes 3145732
  3.7 0.9 %copy-start.3 = (f32[256,256]{1,0:T(8,128)S(1)}, f32[256,256]{1,0:T(8,128)}, u32[]{:S(2)}) copy-start(f32[256,256]{1,0:T(8,128)} %constant.4.clone.fwd_hbm) | copy-start | bytes 786436
  4.6 0.9 %copy-start.4 = (bf16[1,512,128]{2,1,0:T(8,128)(2,1)S(1)}, bf16[1,512,128]{2,1,0:T(8,128)(2,1)}, u32[]{:S(2)}) copy-start(bf16[1,512,128]{2,1,0:T(8,128)(2,1)} %taps_hbm.1) | copy-start | bytes 393220
  5.5 0.9 %copy-start.5 = (bf16[1,127,512]{2,1,0:T(8,128)(2,1)S(1)}, bf16[1,127,512]{2,1,0:T(8,128)(2,1)}, u32[]{:S(2)}) copy-start(bf16[1,127,512]{2,1,0:T(8,128)(2,1)} %tail_hbm.1) | copy-start | bytes 390148
  6.4 0.9 %copy-start.6 = (f32[128,256]{1,0:T(8,128)S(1)}, f32[128,256]{1,0:T(8,128)}, u32[]{:S(2)}) copy-start(f32[128,256]{1,0:T(8,128)} %constant.5.clone.inv_hbm) | copy-start | bytes 393220
  7.3 0.7 %copy-start.7 = (bf16[1,3,3,512]{3,2,1,0:T(4,128)(2,1)S(1)}, bf16[1,3,3,512]{3,2,1,0:T(4,128)(2,1)}, u32[]{:S(2)}) copy-start(bf16[1,3,3,512]{3,2,1,0:T(4,128)(2,1)} %short_hbm.1) | copy-start | bytes 27652
  8.0 0.7 %copy-start.8 = (bf16[1,3,2,512]{3,2,1,0:T(2,128)(2,1)S(1)}, bf16[1,3,2,512]{3,2,1,0:T(2,128)(2,1)}, u32[]{:S(2)}) copy-start(bf16[1,3,2,512]{3,2,1,0:T(2,128)(2,1)} %prior_hbm.1) | copy-start | bytes 18436
  8.7 0.7 %copy-start.9 = (bf16[1,512]{1,0:T(2,128)(2,1)S(1)}, bf16[1,512]{1,0:T(2,128)(2,1)}, u32[]{:S(2)}) copy-start(bf16[1,512]{1,0:T(2,128)(2,1)} %gain_hbm.1) | copy-start | bytes 3076

commit v4 on v3

--- a/solution.py
+++ b/solution.py
@@ -12,7 +12,7 @@
 F32 = jnp.float32
 BF16 = jnp.bfloat16
 CHUNK = 512
-VMEM_BYTES = 40 * 1024 * 1024
+VMEM_BYTES = 64 * 1024 * 1024
 
 
 def transforms(block):
@@ -126,10 +126,10 @@
             ctx=lax.rem(me + step, n_ctx),
         )
 
-    def taps_copy(step, slot):
+    def taps_copy(src, owner, up):
         return remote(
-            taps_hbm.at[0], taps_all.at[slot], taps_send.at[step], taps_recv.at[step],
-            ctx=lax.rem(z + step, rows_of) * 2 + x,
+            src, taps_all.at[owner], taps_send.at[int(up), owner], taps_recv.at[owner],
+            ctx=lax.rem(me + (2 if up else n_ctx - 2), n_ctx),
         )
 
     def tail_copy(part):
@@ -159,8 +159,9 @@
             mixed.at[:, at], out_ref.at[:, at], out_send.at[t], out_recv.at[t], section=after
         )
 
-    def chunk(n):
-        row = lax.rem(z + n // parts, rows_of)
+    def chunk(n, at=z):
+        step = n // parts
+        row = jnp.where(step < rows_of - at, at + step, rows_of - 1 - step)
         part = lax.rem(n, parts)
         return row * parts + part, row, part
 
@@ -175,8 +176,13 @@
         def _():
             msg_copy(step, me).start()
 
-    for step in range(rows_of - 1, 0, -1):
-        taps_copy(step, z).start()
+    @pl.when(z < rows_of - 1)
+    def _():
+        taps_copy(taps_hbm.at[0], z, True).start()
+
+    @pl.when(z > 0)
+    def _():
+        taps_copy(taps_hbm.at[0], z, False).start()
 
     @pl.when(z > 0)
     def _():
@@ -240,7 +246,7 @@
     lax.fori_loop(0, chunks, partner_products, 0)
 
     def own_products(n, carry):
-        slot, row, part = chunk(n + parts)
+        slot, row, part = chunk(n, jnp.minimum(z + 1, rows_of - 1))
         c = 2 * row + x
 
         @pl.when(part == 0)
@@ -298,13 +304,27 @@
         def _():
             hist_copy(p_own, slot).wait_recv()
 
+    def relay(step):
+        below, above = z - step, z + step
+
+        @pl.when(below >= 0)
+        def _():
+            taps_copy(taps_all.at[below], below, True).wait_recv()
+
+            @pl.when(z < rows_of - 1)
+            def _():
+                taps_copy(taps_all.at[below], below, True).start()
+
+        @pl.when(above < rows_of)
+        def _():
+            taps_copy(taps_all.at[above], above, False).wait_recv()
+
+            @pl.when(z > 0)
+            def _():
+                taps_copy(taps_all.at[above], above, False).start()
+
     def respond(n):
         slot, row, part = chunk(n)
-
-        @pl.when((n >= parts) & (part == 0))
-        def _():
-            taps_copy(lax.rem(z - row + rows_of, rows_of), row).wait_recv()
-
         at = pl.ds(pl.multiple_of(part * sub, 128), sub)
         taps = taps_all[row, at, :]
         over = (((1,), (1,)), ((), ()))
@@ -316,36 +336,45 @@
         responses[slot, block:] = response[block:]
 
     def with_product(n, carry):
-        slot, _, _ = chunk(n)
+        slot, _, part = chunk(n)
         p_copy(slot).wait_recv()
 
         @pl.when((x == 0) & (z < rows_of - 1))
         def _():
             hist_copy(p_in, slot).start()
 
+        @pl.when((n >= parts) & (part == 0))
+        def _():
+            relay(n // parts)
+
         respond(n)
 
         @pl.when(x == 0)
         def _():
             give_back(slot, p_own)
 
-        @pl.when(x == 1)
-        def _():
-            keep(n, p_in)
-
-        return carry
-
-    def with_history(n, carry):
+        @pl.when((x == 1) & (n > 0))
+        def _():
+            with_history(n - 1)
+
+        return carry
+
+    def with_history(n):
         slot, _, _ = chunk(n)
         wait_hist(slot)
+        give_back(slot, hist)
+
+    def own_rows(n, carry):
+        slot, _, _ = chunk(n)
 
         @pl.when(x == 0)
         def _():
+            wait_hist(slot)
             keep(n, hist)
 
         @pl.when(x == 1)
         def _():
-            give_back(slot, hist)
+            keep(n, p_in)
 
         return carry
 
@@ -354,7 +383,12 @@
         return carry
 
     lax.fori_loop(0, chunks, with_product, 0)
-    lax.fori_loop(0, chunks, with_history, 0)
+
+    @pl.when(x == 1)
+    def _():
+        with_history(chunks - 1)
+
+    lax.fori_loop(0, chunks, own_rows, 0)
     lax.fori_loop(0, chunks, with_partner, 0)
 
     @pl.when(me < n_ctx - 1)
@@ -363,8 +397,19 @@
 
     for step in range(1, n_ctx):
         msg_copy(step, me).wait_send()
-    for step in range(1, rows_of):
-        taps_copy(step, z).wait_send()
+
+    def drain_taps(owner, carry):
+        @pl.when((owner <= z) & (z < rows_of - 1))
+        def _():
+            taps_copy(taps_all.at[owner], owner, True).wait_send()
+
+        @pl.when((owner >= z) & (z > 0))
+        def _():
+            taps_copy(taps_all.at[owner], owner, False).wait_send()
+
+        return carry
+
+    lax.fori_loop(0, rows_of, drain_taps, 0)
 
     @pl.when(z > 0)
     def _():
@@ -435,7 +480,7 @@
             sems((10,)),
             sems((n_ctx,)),
             sems((n_ctx,)),
-            sems((rows_of,)),
+            sems((2, rows_of)),
             sems((rows_of,)),
             sems((width // sub,)),
             sems((chunks,)),

time: 52.5 us -> 45.5 us (0.87)
  the two profiles are of different devices: /device:TPU:0 before, /device:TPU:26 now
where the time goes in v4:
time: 45.5 us; the launch traced here: 45.3 us
  Pallas kernels  43 us (95%)
  local copies, waits for them, and re-layouts  2.29 us (5%)
    pallas_call x1, Pallas kernels, body(): pl.pallas_call(functools.partial(kernel, n_section, n_ctx), out_shape=jax...  43 us
    unnamed x1, local copies, waits for them, and re-layouts  2.29 us

profile of v4, /device:TPU:26, one launch (start us, length us, event | category | flops | bytes accessed | tf_op | source)
XLA Modules:
  0.0 45.3 jit_solution(8491578027333485471)
XLA Ops:
  0.0 43.0 %paired_filter.1 = bf16[128,4096]{1,0:T(8,128)(2,1)} custom-call(bf16[128,4096]{1,0:T(8,128)(2,1)} %q_hbm.1, bf16[128,4096]{1,0:T(8,128)(2,1)} %k_hbm.1, bf16[128,4096]{1,0:T(8,128)(2,1)} %v_hbm.1, bf16[1,3,3,512]{3,2,1,0:T(4,128)(2,1)} %short_hbm.1, bf16[1,512,128]{2,1,0:T(8,128)(2,1)} %taps_hbm.1, bf16[1,512]{1,0:T(2,128)(2,1)} %gain_hbm.1, ...), custom_call_target="tpu_custom_call" | custom-call | flops 1073741824 | bytes 6291456 | tf_op jit(solution)/shard_map/paired_filter/pallas_call | solution.py:448
  43.0 2.3 %copy.12 = bf16[128,4096]{1,0:T(8,128)(2,1)} copy(bf16[128,4096]{1,0:T(8,128)(2,1)} %paired_filter.1) | data formatting | bytes 2097152

commit v5 on v4

--- a/solution.py
+++ b/solution.py
@@ -11,7 +11,7 @@
 MESH = pl.DeviceIdType.MESH
 F32 = jnp.float32
 BF16 = jnp.bfloat16
-CHUNK = 512
+CHUNK = 256
 VMEM_BYTES = 64 * 1024 * 1024
 
 
@@ -353,9 +353,13 @@
         def _():
             give_back(slot, p_own)
 
-        @pl.when((x == 1) & (n > 0))
-        def _():
-            with_history(n - 1)
+        @pl.when(x == 1)
+        def _():
+            keep(n, p_in)
+
+            @pl.when(n > 0)
+            def _():
+                with_history(n - 1)
 
         return carry
 
@@ -367,15 +371,8 @@
     def own_rows(n, carry):
         slot, _, _ = chunk(n)
 
-        @pl.when(x == 0)
-        def _():
-            wait_hist(slot)
-            keep(n, hist)
-
-        @pl.when(x == 1)
-        def _():
-            keep(n, p_in)
-
+        wait_hist(slot)
+        keep(n, hist)
         return carry
 
     def with_partner(n, carry):
@@ -388,7 +385,10 @@
     def _():
         with_history(chunks - 1)
 
-    lax.fori_loop(0, chunks, own_rows, 0)
+    @pl.when(x == 0)
+    def _():
+        lax.fori_loop(0, chunks, own_rows, 0)
+
     lax.fori_loop(0, chunks, with_partner, 0)
 
     @pl.when(me < n_ctx - 1)

time: 45.5 us -> 44.7 us (0.982)
  the two profiles are of different devices: /device:TPU:26 before, /device:TPU:0 now
where the time goes in v5:
time: 44.7 us; the launch traced here: 44.5 us
  Pallas kernels  42.2 us (94%)
  local copies, waits for them, and re-layouts  2.29 us (5%)
    pallas_call x1, Pallas kernels, body(): pl.pallas_call(functools.partial(kernel, n_section, n_ctx), out_shape=jax...  42.2 us
    unnamed x1, local copies, waits for them, and re-layouts  2.29 us

profile of v5, /device:TPU:0, one launch (start us, length us, event | category | flops | bytes accessed | tf_op | source)
XLA Modules:
  0.0 44.5 jit_solution(14341756230541698356)
XLA Ops:
  0.0 42.2 %paired_filter.1 = bf16[128,4096]{1,0:T(8,128)(2,1)} custom-call(bf16[128,4096]{1,0:T(8,128)(2,1)} %q_hbm.1, bf16[128,4096]{1,0:T(8,128)(2,1)} %k_hbm.1, bf16[128,4096]{1,0:T(8,128)(2,1)} %v_hbm.1, bf16[1,3,3,512]{3,2,1,0:T(4,128)(2,1)} %short_hbm.1, bf16[1,512,128]{2,1,0:T(8,128)(2,1)} %taps_hbm.1, bf16[1,512]{1,0:T(2,128)(2,1)} %gain_hbm.1, ...), custom_call_target="tpu_custom_call" | custom-call | flops 1073741824 | bytes 6291456 | tf_op jit(solution)/shard_map/paired_filter/pallas_call | solution.py:448
  42.2 2.3 %copy.12 = bf16[128,4096]{1,0:T(8,128)(2,1)} copy(bf16[128,4096]{1,0:T(8,128)(2,1)} %paired_filter.1) | data formatting | bytes 2097152

commit v6 on v5

--- a/solution.py
+++ b/solution.py
@@ -11,8 +11,8 @@
 MESH = pl.DeviceIdType.MESH
 F32 = jnp.float32
 BF16 = jnp.bfloat16
-CHUNK = 256
-VMEM_BYTES = 64 * 1024 * 1024
+CHUNK = 512
+VMEM_BYTES = 62 * 1024 * 1024
 
 
 def transforms(block):
@@ -38,7 +38,7 @@
     n_section, n_ctx,
     q_hbm, k_hbm, v_hbm, short_hbm, taps_hbm, gain_hbm, prior_hbm, tail_hbm, fwd_hbm, inv_hbm,
     out_ref,
-    q_ref, k_ref, v_ref, short_ref, gain_ref, prior_ref, tail_ref, fwd_f32, inv_f32, fwd_ref, inv_ref, own_msg, msgs, taps_all, own_tail, edge_out, edge_in, edges,
+    q_ref, k_ref, v_ref, short_ref, gain_ref, prior_ref, tail_ref, fwd_f32, inv_f32, fwd_ref, resp_ref, inv_ref, own_msg, msgs, taps_all, own_tail, edge_out, edge_in, edges,
     p_out, p_own, p_in, hist, responses, f_out, f_in, mixed,
     load_sem, msg_send, msg_recv, taps_send, taps_recv, tail_send, hist_send, hist_recv,
     edge_send, edge_recv, p_send, p_recv, f_send, f_recv, out_send, out_recv,
@@ -189,6 +189,30 @@
         for part in range(parts):
             tail_copy(part).start()
 
+    def respond(n):
+        slot, row, part = chunk(n)
+        at = pl.ds(pl.multiple_of(part * sub, 128), sub)
+        taps = taps_all[row, at, :]
+        response = lax.dot_general(
+            resp_ref[...],
+            jnp.concatenate([taps, taps], axis=1),
+            (((1,), (1,)), ((), ())),
+            preferred_element_type=F32,
+        )
+        gain = msgs[2 * row + x, :, at].astype(F32)[15:16]
+        responses[slot, :block] = response[:block] + gain
+        responses[slot, block:] = response[block:]
+
+    for load in loads[7:]:
+        load.wait()
+    high, low = two_terms(fwd_f32[...])
+    fwd_ref[...] = jnp.concatenate([high, low], axis=1)
+    resp_ref[...] = jnp.concatenate([high[:, :block], low[:, :block]], axis=1)
+    high, low = two_terms(inv_f32[...])
+    inv_ref[...] = jnp.concatenate([high, low, high], axis=1)
+    for part in range(parts):
+        respond(part)
+
     def wait_msg(c):
         @pl.when(c != me)
         def _():
@@ -210,11 +234,12 @@
         rows = ref[:, at].astype(F32)
         ends = edges[0:6, at]
         older, newer = ends[2 * m : 2 * m + 1], ends[2 * m + 1 : 2 * m + 2]
-        place = lax.broadcasted_iota(jnp.int32, rows.shape, 0)
-        one = jnp.where(place == 0, newer, pltpu.roll(rows, 1, 0))
-        two = jnp.where(
-            place == 0, older, jnp.where(place == 1, newer, pltpu.roll(rows, 2, 0))
-        )
+        one, two = pltpu.roll(rows, 1, 0), pltpu.roll(rows, 2, 0)
+        place = lax.broadcasted_iota(jnp.int32, (8, 128), 0)
+        first = jnp.where(place == 0, newer, one[:8])
+        second = jnp.where(place == 0, older, jnp.where(place == 1, newer, two[:8]))
+        one = jnp.concatenate([first, one[8:]], axis=0)
+        two = jnp.concatenate([second, two[8:]], axis=0)
         taps = weights[3 * m : 3 * m + 3]
         return taps[0:1] * rows + taps[1:2] * one + taps[2:3] * two
 
@@ -263,10 +288,6 @@
         return carry
 
     lax.fori_loop(0, chunks, own_products, 0)
-    for load in loads[7:]:
-        load.wait()
-    fwd_ref[0], fwd_ref[1] = two_terms(fwd_f32[...])
-    inv_ref[0], inv_ref[1] = two_terms(inv_f32[...])
 
     def finish(c, part, filtered):
         for lane, at, weights in lanes(c, part):
@@ -279,17 +300,14 @@
         f_copy(slot).wait_recv()
         finish(2 * row + 1 - x, part, f_in[slot].astype(F32))
 
-    def spectrum(window):
-        return dot(fwd_ref[0], window) + dot(fwd_ref[1], window)
-
     def filtered_block(slot, before_ref, current_ref):
-        window = jnp.concatenate([before_ref[slot], current_ref[slot]], axis=0)
-        waves = spectrum(window)
+        window = [before_ref[slot], current_ref[slot]]
+        waves = dot(fwd_ref[...], jnp.concatenate(window + window, axis=0))
         one, two = waves[:block], waves[block:]
         real, imag = responses[slot, :block], responses[slot, block:]
         result = jnp.concatenate([one * real - two * imag, one * imag + two * real], axis=0)
         high, low = two_terms(result)
-        return dot(inv_ref[0], high) + (dot(inv_ref[1], high) + dot(inv_ref[0], low))
+        return dot(inv_ref[...], jnp.concatenate([high, high, low], axis=0))
 
     def give_back(slot, before_ref):
         f_out[slot] = filtered_block(slot, before_ref, p_in).astype(BF16)
@@ -323,18 +341,6 @@
             def _():
                 taps_copy(taps_all.at[above], above, False).start()
 
-    def respond(n):
-        slot, row, part = chunk(n)
-        at = pl.ds(pl.multiple_of(part * sub, 128), sub)
-        taps = taps_all[row, at, :]
-        over = (((1,), (1,)), ((), ()))
-        response = lax.dot_general(
-            fwd_ref[0, :, :block], taps, over, preferred_element_type=F32
-        ) + lax.dot_general(fwd_ref[1, :, :block], taps, over, preferred_element_type=F32)
-        gain = msgs[2 * row + x, :, at].astype(F32)[15:16]
-        responses[slot, :block] = response[:block] + gain
-        responses[slot, block:] = response[block:]
-
     def with_product(n, carry):
         slot, _, part = chunk(n)
         p_copy(slot).wait_recv()
@@ -347,7 +353,9 @@
         def _():
             relay(n // parts)
 
-        respond(n)
+        @pl.when(n >= parts)
+        def _():
+            respond(n)
 
         @pl.when(x == 0)
         def _():
@@ -447,7 +455,7 @@
     sems = pltpu.SemaphoreType.DMA
     return pl.pallas_call(
         functools.partial(kernel, n_section, n_ctx),
-        out_shape=jax.ShapeDtypeStruct(query.shape, BF16),
+        out_shape=pltpu.VMEM(query.shape, BF16),
         in_specs=[hbm] * 10,
         out_specs=pl.BlockSpec(memory_space=pl.ANY),
         scratch_shapes=[
@@ -460,8 +468,9 @@
             pltpu.VMEM(prior_product.shape, BF16),
             pltpu.VMEM(forward.shape, F32),
             pltpu.VMEM(inverse.shape, F32),
-            pltpu.VMEM((2,) + forward.shape, BF16),
-            pltpu.VMEM((2,) + inverse.shape, BF16),
+            pltpu.VMEM((2 * block, 4 * block), BF16),
+            pltpu.VMEM((2 * block, 2 * block), BF16),
+            pltpu.VMEM((block, 6 * block), BF16),
             pltpu.VMEM((16, width), BF16),
             pltpu.VMEM((n_ctx, 16, width), BF16),
             pltpu.VMEM((rows_of, width, block), BF16),

time: 44.7 us -> 41.9 us (0.937)
  Pallas kernels: 42.2 us -> 40.7 us
  local copies, waits for them, and re-layouts: 2.29 us -> 0.97 us
    pallas_call x1, Pallas kernels: 42.2 us -> 40.7 us  [body(): pl.pallas_call(functools.partial(kernel, n_section, n_ctx), out_shape=plt...]
    unnamed x1, local copies, waits for them, and re-layouts: 2.29 us -> 0.97 us
where the time goes in v6:
time: 41.9 us; the launch traced here: 41.7 us
  Pallas kernels  40.7 us (97%)
  local copies, waits for them, and re-layouts  0.97 us (2%)
    pallas_call x1, Pallas kernels, body(): pl.pallas_call(functools.partial(kernel, n_section, n_ctx), out_shape=plt...  40.7 us
    unnamed x1, local copies, waits for them, and re-layouts  0.97 us

profile of v6, /device:TPU:0, one launch (start us, length us, event | category | flops | bytes accessed | tf_op | source)
XLA Modules:
  0.0 41.7 jit_solution(16301551767142697020)
XLA Ops:
  0.0 40.7 %paired_filter.1 = bf16[128,4096]{1,0:T(8,128)(2,1)S(1)} custom-call(bf16[128,4096]{1,0:T(8,128)(2,1)} %q_hbm.1, bf16[128,4096]{1,0:T(8,128)(2,1)} %k_hbm.1, bf16[128,4096]{1,0:T(8,128)(2,1)} %v_hbm.1, bf16[1,3,3,512]{3,2,1,0:T(4,128)(2,1)} %short_hbm.1, bf16[1,512,128]{2,1,0:T(8,128)(2,1)} %taps_hbm.1, bf16[1,512]{1,0:T(2,128)(2,1)} %gain_hbm.1, ...), custom_call_target="tpu_custom_call" | custom-call | flops 1073741824 | bytes 6291456 | tf_op jit(solution)/shard_map/paired_filter/pallas_call | solution.py:456
  40.7 1.0 %copy.12 = bf16[128,4096]{1,0:T(8,128)(2,1)} copy(bf16[128,4096]{1,0:T(8,128)(2,1)S(1)} %paired_filter.1) | data formatting | bytes 2097152

commit v7 on v6

--- a/solution.py
+++ b/solution.py
@@ -115,15 +115,18 @@
         )
 
     chunks = rows_of * parts
-    partner_step = lax.rem(partner - me + n_ctx, n_ctx)
 
     def edge_copy():
         return remote(edge_out, edge_in, edge_send, edge_recv, ctx=lax.rem(me + 1, n_ctx))
 
-    def msg_copy(step, slot):
-        return remote(
-            own_msg, msgs.at[slot], msg_send.at[step], msg_recv.at[step],
-            ctx=lax.rem(me + step, n_ctx),
+    def msg_copy(src, owner, sem, target):
+        return remote(src, msgs.at[owner], msg_send.at[sem], msg_recv.at[owner], ctx=target)
+
+    def msg_copies(step):
+        target = lax.rem(me + 2 * step, n_ctx)
+        return (
+            msg_copy(own_msg, me, step, target),
+            msg_copy(msgs.at[partner], partner, rows_of - 1 + step, target),
         )
 
     def taps_copy(src, owner, up):
@@ -169,12 +172,9 @@
     def _():
         edge_copy().start()
 
-    msg_copy(partner_step, me).start()
-    for step in range(n_ctx - 1, 0, -1):
-
-        @pl.when(step != partner_step)
-        def _():
-            msg_copy(step, me).start()
+    msg_copy(own_msg, me, 0, partner).start()
+    for step in range(1, rows_of):
+        msg_copies(step)[0].start()
 
     @pl.when(z < rows_of - 1)
     def _():
@@ -214,9 +214,13 @@
         respond(part)
 
     def wait_msg(c):
-        @pl.when(c != me)
-        def _():
-            msg_copy(lax.rem(me - c + n_ctx, n_ctx), c).wait_recv()
+        @pl.when((c != me) & (c != partner))
+        def _():
+            msg_copy(own_msg, c, 0, partner).wait_recv()
+
+    msg_copy(own_msg, partner, 0, partner).wait_recv()
+    for step in range(1, rows_of):
+        msg_copies(step)[1].start()
 
     @pl.when(me > 0)
     def _():
@@ -255,30 +259,22 @@
             value = feature(v_ref, at, 2, weights)
             dst[slot, :, lane : lane + 128] = (key * value).astype(BF16)
 
-    def partner_products(n, carry):
+    def ready(c, part):
+        @pl.when(part == 0)
+        def _():
+            wait_msg(c)
+            place_edge(c)
+
+    def products(n, carry):
         slot, row, part = chunk(n)
         c = 2 * row + 1 - x
-
-        @pl.when(part == 0)
-        def _():
-            wait_msg(c)
-            place_edge(c)
-
+        ready(c, part)
         product(c, part, p_out, slot)
         p_copy(slot).start()
-        return carry
-
-    lax.fori_loop(0, chunks, partner_products, 0)
-
-    def own_products(n, carry):
+
         slot, row, part = chunk(n, jnp.minimum(z + 1, rows_of - 1))
         c = 2 * row + x
-
-        @pl.when(part == 0)
-        def _():
-            wait_msg(c)
-            place_edge(c)
-
+        ready(c, part)
         product(c, part, p_own, slot)
 
         @pl.when((x == 1) & (z < rows_of - 1))
@@ -287,7 +283,7 @@
 
         return carry
 
-    lax.fori_loop(0, chunks, own_products, 0)
+    lax.fori_loop(0, chunks, products, 0)
 
     def finish(c, part, filtered):
         for lane, at, weights in lanes(c, part):
@@ -403,8 +399,10 @@
     def _():
         edge_copy().wait_send()
 
-    for step in range(1, n_ctx):
-        msg_copy(step, me).wait_send()
+    msg_copy(own_msg, me, 0, partner).wait_send()
+    for step in range(1, rows_of):
+        for copy in msg_copies(step):
+            copy.wait_send()
 
     def drain_taps(owner, carry):
         @pl.when((owner <= z) & (z < rows_of - 1))

time: 41.9 us -> 45.3 us (1.081)
  Pallas kernels: 40.7 us -> 44.1 us
    pallas_call x1, Pallas kernels: 40.7 us -> 44.1 us  [body(): pl.pallas_call(functools.partial(kernel, n_section, n_ctx), out_shape=plt...]
where the time goes in v7:
time: 45.3 us; the launch traced here: 45.1 us
  Pallas kernels  44.1 us (97%)
  local copies, waits for them, and re-layouts  0.97 us (2%)
    pallas_call x1, Pallas kernels, body(): pl.pallas_call(functools.partial(kernel, n_section, n_ctx), out_shape=plt...  44.1 us
    unnamed x1, local copies, waits for them, and re-layouts  0.97 us

profile of v7, /device:TPU:0, one launch (start us, length us, event | category | flops | bytes accessed | tf_op | source)
XLA Modules:
  0.0 45.1 jit_solution(6515771491433146632)
XLA Ops:
  0.0 44.1 %paired_filter.1 = bf16[128,4096]{1,0:T(8,128)(2,1)S(1)} custom-call(bf16[128,4096]{1,0:T(8,128)(2,1)} %q_hbm.1, bf16[128,4096]{1,0:T(8,128)(2,1)} %k_hbm.1, bf16[128,4096]{1,0:T(8,128)(2,1)} %v_hbm.1, bf16[1,3,3,512]{3,2,1,0:T(4,128)(2,1)} %short_hbm.1, bf16[1,512,128]{2,1,0:T(8,128)(2,1)} %taps_hbm.1, bf16[1,512]{1,0:T(2,128)(2,1)} %gain_hbm.1, ...), custom_call_target="tpu_custom_call" | custom-call | flops 1073741824 | bytes 6291456 | tf_op jit(solution)/shard_map/paired_filter/pallas_call | solution.py:454
  44.2 1.0 %copy.12 = bf16[128,4096]{1,0:T(8,128)(2,1)} copy(bf16[128,4096]{1,0:T(8,128)(2,1)S(1)} %paired_filter.1) | data formatting | bytes 2097152
